TPU v7x, 128 devices: a whole 4x4x4 slice. The times are simulated.
128 devices in a mesh: tm: 4 (over z_lo, core), chan: 32 (over x, z_hi, y).
Axes of the slice: x: 4, y: 4, z: 4 (z_hi: 2, z_lo: 2; z = z_hi * 2 + z_lo), core: 2. Of those that a mesh axis runs over, the one named last changes fastest.
Arguments:
- samples: float32 [24, 1024, 8192], P('tm', 'chan'), may hold values from -48 to 48
- source_index: int32 [128], replicated, may hold values from 0 to 8191, as said below
- dead_flags: int32 [8192], replicated, may hold values 0 or 1
Outputs:
- stacks: bfloat16 [512, 2, 128, 8192], P('tm', None, None, 'chan')
Inputs may be any that keep to these rules, and one draw needn't show every extreme that they name: `source_index`: 128 distinct channel numbers in no particular order; channels 0 and 8191 are always among them. `dead_flags`: 1 marks a dead channel.
All inputs are finite; a program needn't handle non-finite values.
Results may differ from a plain program's by a relative error of at most 0.0057.
Values may be sent and summed in bfloat16 or wider, within the bound.
No kernel may reach another device: no remote copies, remote signals or barrier semaphores. Data moves between devices by JAX's collectives and lax.ppermute only.
A program may use at most 192 MiB of HBM per device.

v0:
```python
import math

import jax
import jax.numpy as jnp
from jax import lax
from jax.sharding import PartitionSpec as P

WIN = 1024
BINS = 512
BAND = 64


whiten_eps = 1e-06


def dft_table(row_count, bin_count):
    sample = jnp.arange(row_count, dtype=jnp.int32)
    frequency = jnp.arange(bin_count, dtype=jnp.int32)
    angles = (sample[:, None] * frequency[None, :] % WIN).astype(jnp.float32) * (
        2.0 * math.pi / WIN
    )
    window_taper = 0.5 - 0.5 * jnp.cos((sample.astype(jnp.float32) + 0.5) * (2.0 * math.pi / WIN))
    return jnp.concatenate(
        [window_taper[:, None] * jnp.cos(angles), -window_taper[:, None] * jnp.sin(angles)], axis=1
    )


def whiten(spectrum, live):
    halves = spectrum.reshape(spectrum.shape[0], 2, -1, BAND, spectrum.shape[2])
    band_power = jnp.sum(halves * halves, axis=(1, 3)) / BAND
    factor = live[None, None, :] / jnp.sqrt(band_power + whiten_eps)
    whitened = halves * factor[:, None, :, None, :]
    return whitened.reshape(spectrum.shape[0], 2, spectrum.shape[1] // 2, spectrum.shape[2]).astype(
        jnp.bfloat16
    )


def transform(blocks, dft_rows, live):
    spectrum = jnp.einsum(
        "kwc,wg->kgc",
        blocks,
        dft_rows,
        precision=lax.Precision.HIGHEST,
        preferred_element_type=jnp.float32,
    )
    return whiten(spectrum, live)


def shards(samples, source_index, dead_flags):
    chan_count = lax.axis_size("chan")
    channels = samples.shape[2]
    block_width = channels // chan_count
    chan_start = lax.axis_index("chan") * block_width
    live_all = 1.0 - dead_flags.astype(jnp.float32)
    live_own = lax.dynamic_slice_in_dim(live_all, chan_start, block_width)
    full_table = dft_table(WIN, BINS)
    white_local = transform(
        lax.all_to_all(samples, "chan", split_axis=2, concat_axis=1, tiled=True),
        full_table,
        live_own,
    )
    whitened = lax.all_to_all(white_local, "tm", split_axis=2, concat_axis=0, tiled=True)
    window_count = whitened.shape[0]
    chooser = (
        source_index[None, :] == chan_start + jnp.arange(block_width, dtype=jnp.int32)[:, None]
    ).astype(jnp.bfloat16)
    partial_value = jnp.einsum(
        "kpfc,cs->kpfs", whitened, chooser, preferred_element_type=jnp.float32
    )
    source = lax.psum(partial_value.astype(jnp.bfloat16), "chan")
    real_part = source[:, 0]
    imag_part = source[:, 1]
    left_side = jnp.stack(
        [jnp.stack([real_part, imag_part], 0), jnp.stack([imag_part, -real_part], 0)], 0
    )
    product = jnp.einsum(
        "apkfs,kpfc->fasc", left_side, whitened, preferred_element_type=jnp.float32
    )
    return (product / window_count).astype(jnp.bfloat16)


def solution(mesh):
    return jax.shard_map(
        shards,
        mesh=mesh,
        in_specs=(P("tm", "chan", None), P(), P()),
        out_specs=P("tm", None, None, "chan"),
        check_vma=False,
    )
```

profile of v0, /device:TPU:0, one launch (start us, length us, event | category | flops | bytes accessed | tf_op | source)
XLA Modules:
  0.0 706.5 jit_solution(3619632084827637040)
XLA Ops:
  6.5 17.6 %copy.24 = f32[6,32,8192]{1,0,2:T(8,128)} copy(f32[6,32,8192]{2,1,0:T(8,128)} %param.3) | data formatting | bytes 12582912 | tf_op args[0]
  24.1 29.9 %reshape.48 = f32[32,1,49152]{2,1,0:T(1,128)} reshape(f32[8192,6,32]{2,1,0:T(8,128)} %bitcast.48) | data formatting | bytes 12582912
  54.1 10.8 %all-to-all-start = ((f32[32,1,49152]{2,1,0:T(1,128)}), f32[32,1,49152]{2,1,0:T(1,128)}, u32[]{:S(2)}, u32[]{:S(2)}) async-start(f32[32,1,49152]{2,1,0:T(1,128)} %reshape.48), calls=%async_computation | async-start | bytes 12582912 | tf_op jit(solution)/shard_map/all_to_all | solution.py:58
  64.9 0.8 fusion.17
  65.8 9.3 %sine_multiply_fusion = (f32[1024,512]{0,1:T(8,128)S(1)}, f32[1024,512]{0,1:T(8,128)}) fusion(f32[1024]{0:T(1024)S(1)} %fusion.16, f32[1024]{0:T(1024)S(1)} %multiply_subtract_fusion), kind=kLoop, calls=%fused_computation.17 | loop fusion | flops 8388608 | bytes 4202496 | tf_op jit(solution)/shard_map/mul | solution.py:24
  75.0 96.8 %all-to-all-done = f32[32,1,49152]{2,1,0:T(1,128)} async-done(((f32[32,1,49152]{2,1,0:T(1,128)}), f32[32,1,49152]{2,1,0:T(1,128)}, u32[]{:S(2)}, u32[]{:S(2)}) %all-to-all-start) | async-done | bytes 6291488 | tf_op jit(solution)/shard_map/all_to_all | solution.py:58
  171.9 0.6 broadcast.70
  172.4 19.4 %reduce = f32[32,49152]{1,0:T(8,128)} reduce(f32[32,1,49152]{2,1,0:T(1,128)} %all-to-all-done, f32[]{:T(128)} %broadcast.70), dimensions={1}, to_apply=%all_to_all.26.reduce_sub_computation | reduce | bytes 12582916 | tf_op jit(solution)/shard_map/all_to_all | solution.py:58
  191.9 30.5 %reshape.49 = f32[8192,6,32]{2,1,0:T(8,128)} reshape(f32[32,49152]{1,0:T(8,128)} %reduce) | data formatting | bytes 12582912
  222.4 19.4 %copy.25 = f32[6,32,32,256]{3,1,2,0:T(8,128)} copy(f32[6,32,32,256]{1,0,3,2:T(8,128)} %bitcast.47) | data formatting | bytes 12582912 | tf_op jit(solution)/shard_map/all_to_all | solution.py:58
  241.8 24.3 %bitcast_multiply_fusion.1 = (f32[6,1024,256]{2,1,0:T(8,128)}, f32[1024,6,256]{2,0,1:T(8,128)}) fusion(f32[6,1024,256]{2,1,0:T(8,128)} %bitcast.51, f32[1024,512]{0,1:T(8,128)S(1)} %get-tuple-element.11, f32[1024,512]{0,1:T(8,128)} %get-tuple-element.12), kind=kOutput, calls=%fused_computation.2 | convolution fusion | flops 19329974272 | bytes 23068672 | tf_op jit(solution)/shard_map/kwc,wg->kgc/dot_general | solution.py:39
  266.1 3.5 reduce_sum.9
  269.7 0.2 mul.107
  269.9 3.6 multiply_convert_fusion
  273.5 4.9 copy.26
  278.4 3.7 all-to-all-start.1
  282.1 0.0 all-reduce.2.cloned.1.call-start
  282.2 36.8 %all-to-all-done.1 = bf16[6,2,512,256]{3,1,0,2:T(2,128)(2,1)S(1)} async-done(((bf16[6,2,512,256]{3,1,0,2:T(2,128)(2,1)}), bf16[6,2,512,256]{3,1,0,2:T(2,128)(2,1)S(1)}, u32[]{:S(2)}, u32[]{:S(2)}) %all-to-all-start.1) | async-done | bytes 3145760 | tf_op jit(solution)/shard_map/all_to_all | solution.py:62
  319.0 0.0 copy-start
  319.0 1.7 copy-done
  320.7 0.0 copy-start.2
  320.7 2.5 copy.27
  323.1 0.0 copy-done.2
  323.1 2.2 convolution_convert_fusion
  325.3 0.0 all-reduce.2.cloned.1.call-update
  325.4 355.9 %all-reduce.2.cloned.1.call-done = bf16[24,2,128,128]{3,2,1,0:T(8,128)(2,1)} async-done(((bf16[24,2,128,128]{3,2,1,0:T(8,128)(2,1)}), bf16[24,2,128,128]{3,2,1,0:T(8,128)(2,1)}) %all-reduce.2.cloned.1.call-update) | async-done | bytes 1572880 | tf_op jit(solution)/shard_map/psum | solution.py:70
  681.3 0.0 copy-start.1
  681.3 1.7 slice_bitcast_fusion.1
  683.0 0.2 copy-done.1
  683.2 0.1 fusion.19
  683.3 0.3 maximum_bitcast_fusion.2
  683.6 0.3 pad_maximum_fusion
  683.9 15.8 %fusion = bf16[128,2,128,256]{3,2,1,0:T(8,128)(2,1)} fusion(bf16[24,2,128,256,1]{3,2,1,0,4:T(8,128)(2,1)S(1)} %bitcast.50, bf16[2,2,24,128,128]{4,3,2,1,0:T(8,128)(2,1)S(1)} %pad_maximum_fusion), kind=kOutput, calls=%fused_computation.1 | convolution fusion | flops 822083584 | bytes 23068672 | tf_op jit(solution)/shard_map/apkfs,kpfc->fasc/dot_general | solution.py:76
  (4 shorter events, 0.1 us)
Async XLA Ops:
  54.1 117.8 %all-to-all-start = ((f32[32,1,49152]{2,1,0:T(1,128)}), f32[32,1,49152]{2,1,0:T(1,128)}, u32[]{:S(2)}, u32[]{:S(2)}) async-start(f32[32,1,49152]{2,1,0:T(1,128)} %reshape.48), calls=%async_computation | async-start | bytes 12582912 | tf_op jit(solution)/shard_map/all_to_all | solution.py:58
  278.4 40.6 %all-to-all-start.1 = ((bf16[6,2,512,256]{3,1,0,2:T(2,128)(2,1)}), bf16[6,2,512,256]{3,1,0,2:T(2,128)(2,1)S(1)}, u32[]{:S(2)}, u32[]{:S(2)}) async-start(bf16[6,2,512,256]{3,1,0,2:T(2,128)(2,1)} %copy.26), calls=%async_computation.1 | async-start | bytes 6291456 | tf_op jit(solution)/shard_map/all_to_all | solution.py:62
  282.1 399.2 %all-reduce.2.cloned.1.call-start = ((), (), s32[]{:S(2)}) async-start(), calls=%async_computation.2 | async-start | bytes 3145728 | tf_op jit(solution)/shard_map/psum | solution.py:70
  319.0 1.7 copy-start
  320.7 2.5 copy-start.2
  681.3 1.9 copy-start.1
Sparse Core Ops, SparseCore 0:
  325.5 355.7 all-reduce.1
where the time goes:
time: 708 us; the launch traced here: 707 us
  waiting for transfers between devices  490 us (69%)
  local copies, waits for them, and re-layouts  109 us (15%)
  matrix products  42.3 us (6%)
  other arithmetic  37.4 us (5%)
  starting transfers between devices  14.6 us (2%)
  between operations  13.5 us (2%)
    psum x1, waiting for transfers between devices, shards(): source = lax.psum(partial_value.astype(jnp.bfloat16), 'chan')  356 us
    all_to_all x1, waiting for transfers between devices, shards(): lax.all_to_all(samples, 'chan', split_axis=2, concat_axis=1, tiled=True)  96.8 us
    unnamed x9, local copies, waits for them, and re-layouts  79.9 us
    all_to_all x1, waiting for transfers between devices, shards(): lax.all_to_all(white_local, 'tm', split_axis=2, concat_axis=0, tiled=True)  36.8 us
    dot_general x1, matrix products, transform(): jnp.einsum('kwc,wg->kgc', blocks, dft_rows, precision=lax.Precision.HIGHE...  24.3 us
    all_to_all x2, local copies, waits for them, and re-layouts, shards(): lax.all_to_all(samples, 'chan', split_axis=2, concat_axis=1, tiled=True)  20 us
    all_to_all x1, other arithmetic, shards(): lax.all_to_all(samples, 'chan', split_axis=2, concat_axis=1, tiled=True)  19.4 us
    dot_general x1, matrix products, shards(): jnp.einsum('apkfs,kpfc->fasc', left_side, whitened, preferred_element_typ...  15.8 us
  transfers between devices with their start and end apart: 3, of which 3 were waited for; matrix products, arithmetic and copies ran while one was open for 1% of the time, Pallas kernels for 0%

commit v1 on v0

v1 whole, which is shorter than its diff:
```python
import math

import jax
import jax.numpy as jnp
from jax import lax
from jax.experimental import pallas as pl
from jax.experimental.pallas import tpu as pltpu
from jax.sharding import PartitionSpec as P

WIN = 1024
BINS = 512
BAND = 64
WINDOWS = 24
SOURCES = 128
CHAN = 32
TM = 4
KW = WINDOWS // TM
SUB = WIN // CHAN
WIDTH = 256
PICK = SOURCES // CHAN
DATA = KW * SUB
ROWS = DATA + 16
GROUP = 4
DEPTH = WINDOWS * 2 * GROUP
STEPS = 128.0
TOP = 32767.0
EPS = 1e-06
VMEM = 56 * 1024 * 1024

f32 = jnp.float32
bf16 = jnp.bfloat16


def split(x):
    high = x.astype(bf16)
    return high, (x - high.astype(f32)).astype(bf16)


def dft_table():
    row = jnp.arange(2 * BINS, dtype=jnp.int32)[:, None]
    sample = jnp.arange(WIN, dtype=jnp.int32)[None, :]
    frequency = row // (2 * GROUP) * GROUP + row % GROUP
    part = row // GROUP % 2
    phase = (sample * frequency + part * (WIN // 4)) % WIN
    taper = 0.5 - 0.5 * jnp.cos((sample.astype(f32) + 0.5) * (2.0 * math.pi / WIN))
    table = taper * jnp.cos(phase.astype(f32) * (2.0 * math.pi / WIN))
    table = lax.optimization_barrier(table)
    high = lax.reduce_precision(table, 8, 7)
    return high.astype(bf16), (table - high).astype(bf16)


def scale_of(code):
    return jnp.exp2(code * (1.0 / STEPS)) * (1.0 / TOP)


def encode_kernel(samples, source, out, picked, extra):
    step = pl.program_id(0)
    wide = samples.shape[2]
    blocks = wide // WIDTH

    @pl.when(step == 0)
    def _():
        picked[...] = jnp.zeros_like(picked)
        extra[...] = jnp.zeros_like(extra)

    codes = []
    scales = []
    for w in range(KW):
        x = samples[w]
        peak = jnp.max(jnp.abs(x), axis=0, keepdims=True)
        scale = jnp.ceil(jnp.log2(jnp.maximum(peak, 1e-30)) * STEPS) + 1.0
        q = jnp.round(x * (jnp.exp2(scale * (-1.0 / STEPS)) * TOP))
        codes.append(q)
        scales.append(scale)
        qi = q.astype(jnp.int32).astype(jnp.int16)
        for k in range(blocks):
            out[step * blocks + k, w * SUB : (w + 1) * SUB, :] = qi[:, k * WIDTH : (k + 1) * WIDTH]
    scales.append(jnp.zeros((8 - KW, wide), f32))
    scale_rows = jnp.concatenate(scales, 0)
    for k in range(blocks):
        start = pl.multiple_of((step * blocks + k) * 16 + 8, 8)
        for half in range(2):
            lane = k * WIDTH + half * 128
            extra[half, pl.ds(start, 8), :] = scale_rows[:, lane : lane + 128]
    both = jnp.concatenate(codes + [scale_rows, jnp.zeros((8, wide), f32)], 0)
    high = jnp.round(both * (1.0 / 256.0))
    low = both - high * 256.0
    number = lax.broadcasted_iota(jnp.int32, (SOURCES, wide), 1) + step * wide
    chooser = jnp.where(source[...] == number, 1.0, 0.0).astype(bf16)
    over = (((1,), (1,)), ((), ()))
    picked[:, :ROWS] += 256.0 * lax.dot_general(
        chooser, high.astype(bf16), over, preferred_element_type=f32
    ) + lax.dot_general(chooser, low.astype(bf16), over, preferred_element_type=f32)

    @pl.when(step == pl.num_programs(0) - 1)
    def _():
        for half in range(2):
            lanes = slice(half * 128, half * 128 + 128)
            for k in range(PICK):
                extra[half, pl.ds(k, CHAN, stride=16), :] = picked[
                    k * CHAN : (k + 1) * CHAN, lanes
                ]
            rows = extra[half].reshape(CHAN, 16, 128)
            out[:, DATA:, lanes] = rows.astype(jnp.int32).astype(jnp.int16)


def encode(samples, source_index):
    wide = 1024
    return pl.pallas_call(
        encode_kernel,
        grid=(samples.shape[2] // wide,),
        in_specs=[
            pl.BlockSpec((KW, SUB, wide), lambda i: (0, 0, i)),
            pl.BlockSpec((SOURCES, 1), lambda i: (0, 0)),
        ],
        out_specs=pl.BlockSpec((CHAN, ROWS, WIDTH), lambda i: (0, 0, 0)),
        out_shape=jax.ShapeDtypeStruct((CHAN, ROWS, WIDTH), jnp.int16),
        scratch_shapes=[
            pltpu.VMEM((SOURCES, WIDTH), f32),
            pltpu.VMEM((2, CHAN * 16, 128), f32),
        ],
        compiler_params=pltpu.CompilerParams(vmem_limit_bytes=VMEM),
        name="encode",
    )(samples, source_index.reshape(SOURCES, 1))


def transform_kernel(mine, codes, extra, high, low, live, *rest):
    outs, (table, scale) = rest[:TM], rest[TM:]
    w = pl.program_id(0)
    rows = 2 * BAND

    @pl.when(w == 0)
    def _():
        for k in range(TM):
            other = jnp.bitwise_xor(mine[0], k)
            table[k * rows : (k + 1) * rows, :] = high[other, 0]
            table[(TM + k) * rows : (TM + k + 1) * rows, :] = low[other, 0]
        scale[...] = scale_of(extra[:, 8:, :].astype(jnp.int32).astype(f32))

    x = codes[...].astype(jnp.int32).astype(f32) * scale[:, pl.ds(w, 1), :]
    x_high, x_low = split(x.reshape(WIN, WIDTH))
    y = jnp.dot(table[...], x_high, preferred_element_type=f32)
    z = jnp.dot(table[: TM * rows, :], x_low, preferred_element_type=f32)
    for k in range(TM):
        part = slice(k * rows, (k + 1) * rows)
        value = y[part] + (y[(TM + k) * rows : (TM + k + 1) * rows] + z[part])
        power = jnp.sum(value * value, axis=0, keepdims=True) * (1.0 / BAND)
        outs[k][0] = (value * (live[...] * lax.rsqrt(power + EPS))).astype(bf16)


def transform(mine, received, high, low, live, band):
    rows = 2 * BAND
    shape = jax.ShapeDtypeStruct((KW, rows, WIDTH), bf16)
    return pl.pallas_call(
        transform_kernel,
        grid_spec=pltpu.PrefetchScalarGridSpec(
            num_scalar_prefetch=1,
            grid=(KW,),
            in_specs=[
                pl.BlockSpec((CHAN, SUB, WIDTH), lambda w, _: (0, w, 0)),
                pl.BlockSpec((CHAN, 16, WIDTH), lambda w, _: (0, DATA // 16, 0)),
                pl.BlockSpec((TM, 1, rows, WIN), lambda w, _: (0, band, 0, 0)),
                pl.BlockSpec((TM, 1, rows, WIN), lambda w, _: (0, band, 0, 0)),
                pl.BlockSpec((1, WIDTH), lambda w, _: (0, 0)),
            ],
            out_specs=[pl.BlockSpec((1, rows, WIDTH), lambda w, _: (w, 0, 0))] * TM,
            scratch_shapes=[
                pltpu.VMEM((2 * TM * rows, WIN), bf16),
                pltpu.VMEM((CHAN, 8, WIDTH), f32),
            ],
        ),
        out_shape=[shape] * TM,
        compiler_params=pltpu.CompilerParams(vmem_limit_bytes=VMEM),
        name="transform",
    )(
        mine,
        received,
        received,
        high.reshape(TM, 2, rows, WIN),
        low.reshape(TM, 2, rows, WIN),
        live,
    )


def sources_kernel(mine, x, high, low, live, *outs):
    x_high, x_low = split(x[...])
    over = (((1,), (1,)), ((), ()))
    rows = 2 * BINS // TM
    for k in range(TM):
        part = pl.ds(pl.multiple_of(jnp.bitwise_xor(mine[0], k) * rows, rows), rows)
        t_high = high[part, :]
        value = lax.dot_general(x_high, t_high, over, preferred_element_type=f32) + (
            lax.dot_general(x_high, low[part, :], over, preferred_element_type=f32)
            + lax.dot_general(x_low, t_high, over, preferred_element_type=f32)
        )
        for b in range(rows // (2 * BAND)):
            band = value[:, b * 2 * BAND : (b + 1) * 2 * BAND]
            power = jnp.sum(band * band, axis=1, keepdims=True) * (1.0 / BAND)
            outs[k][:, b * 2 * BAND : (b + 1) * 2 * BAND] = (
                band * (live[...] * lax.rsqrt(power + EPS))
            ).astype(bf16)


def sources(mine, received, high, low, live):
    extra = received[:, DATA : DATA + PICK, :].astype(f32)
    codes = extra[:, :, :DATA].reshape(CHAN, PICK, KW, SUB)
    scale = scale_of(extra[:, :, DATA + 0 : DATA + KW])
    x = (codes * scale[..., None]).transpose(2, 1, 0, 3).reshape(KW * PICK, WIN)
    rows = 2 * BINS // TM
    whole = pl.BlockSpec(memory_space=pltpu.VMEM)
    return pl.pallas_call(
        sources_kernel,
        in_specs=[pl.BlockSpec(memory_space=pltpu.SMEM)] + [whole] * 4,
        out_specs=[whole] * TM,
        out_shape=[jax.ShapeDtypeStruct((KW * PICK, rows), bf16)] * TM,
        compiler_params=pltpu.CompilerParams(vmem_limit_bytes=VMEM),
        name="sources",
    )(mine, x, high, low, live)


def arrange_kernel(gathered, out, flat, turned):
    count = TM * KW
    for half in range(2):
        lanes = slice(half * 128, half * 128 + 128)
        flat[half] = gathered[:, :, lanes].reshape(CHAN * count * PICK, 128).astype(f32)
    groups = 4 * BAND // (2 * GROUP)
    for v in range(count):
        for half in range(2):
            both = jnp.concatenate(
                [
                    flat[half, pl.ds(v * PICK + k, CHAN, stride=count * PICK), :]
                    for k in range(PICK)
                ],
                0,
            )
            turned[half * 16 : half * 16 + 16, v * 8 : v * 8 + 8, :] = both.T.reshape(16, 8, SOURCES)
    column = lax.broadcasted_iota(jnp.int32, (DEPTH, 1), 0)
    second = column // GROUP % 2 == 1

    def body(g, carry):
        value = turned[g]
        ahead = pltpu.roll(value, DEPTH - GROUP, 0)
        behind = pltpu.roll(value, GROUP, 0)
        out[g, :SOURCES, :] = value.T.astype(bf16)
        out[g, SOURCES:, :] = jnp.where(second, -behind, ahead).T.astype(bf16)
        return carry

    lax.fori_loop(0, groups, body, 0)


def arrange(gathered):
    groups = 4 * BAND // (2 * GROUP)
    whole = pl.BlockSpec(memory_space=pltpu.VMEM)
    return pl.pallas_call(
        arrange_kernel,
        in_specs=[whole],
        out_specs=whole,
        out_shape=jax.ShapeDtypeStruct((groups, 2 * SOURCES, DEPTH), bf16),
        scratch_shapes=[
            pltpu.VMEM((2, CHAN * TM * KW * PICK, 128), f32),
            pltpu.VMEM((groups, DEPTH, SOURCES), f32),
        ],
        compiler_params=pltpu.CompilerParams(vmem_limit_bytes=VMEM),
        name="arrange",
    )(gathered)


def stack_kernel(left, a, b, c, d, *rest):
    out = rest[-1]
    column = lax.broadcasted_iota(jnp.int32, (2 * SOURCES, DEPTH), 1) % GROUP
    for h in range(2):
        right = jnp.concatenate(
            [v[:, h * 8 : h * 8 + 8, :] for v in [u[...].astype(f32) for u in (a, b, c, d)]], 0
        )
        right = right.reshape(DEPTH, WIDTH).astype(bf16)
        value = left[h]
        for i in range(GROUP):
            mine = jnp.where(column == i, value, jnp.zeros_like(value))
            product = jnp.dot(mine, right, preferred_element_type=f32) * (1.0 / WINDOWS)
            out[h * GROUP + i] = product.reshape(2, SOURCES, WIDTH).astype(bf16)


def stack(left, parts, band, before):
    steps = 2 * BAND // 16
    start = band * steps
    piece = pl.BlockSpec((KW, 16, WIDTH), lambda i: (0, i, 0))
    extra = [] if before is None else [before]
    return pl.pallas_call(
        stack_kernel,
        grid=(steps,),
        in_specs=[pl.BlockSpec((2, 2 * SOURCES, DEPTH), lambda i: (start + i, 0, 0))]
        + [piece] * TM
        + [pl.BlockSpec(memory_space=pl.ANY)] * len(extra),
        out_specs=pl.BlockSpec((2 * GROUP, 2, SOURCES, WIDTH), lambda i: (start + i, 0, 0, 0)),
        out_shape=jax.ShapeDtypeStruct((BINS // TM, 2, SOURCES, WIDTH), bf16),
        input_output_aliases={} if before is None else {5: 0},
        compiler_params=pltpu.CompilerParams(vmem_limit_bytes=VMEM),
        name="stack",
    )(left, *parts, *extra)


def exchange(pieces):
    moved = [pieces[0]]
    for k in range(1, TM):
        moved.append(lax.ppermute(pieces[k], "tm", [(i, i ^ k) for i in range(TM)]))
    return moved


def shards(samples, source_index, dead_flags):
    place = lax.axis_index("chan")
    mine = lax.axis_index("tm").astype(jnp.int32).reshape(1)
    live_all = 1.0 - dead_flags.astype(f32)
    live = lax.dynamic_slice_in_dim(live_all, place * WIDTH, WIDTH).reshape(1, WIDTH)
    own_sources = lax.dynamic_slice_in_dim(source_index.reshape(PICK, CHAN), place, 1, 1)[:, 0]
    live_source = jnp.tile(live_all[own_sources], KW).reshape(KW * PICK, 1)
    high, low = dft_table()

    received = lax.all_to_all(encode(samples, source_index), "chan", 0, 0, tiled=True)
    first = exchange(transform(mine, received, high, low, live, 0))
    spectra = exchange(sources(mine, received, high, low, live_source))
    second = exchange(transform(mine, received, high, low, live, 1))
    gathered = lax.all_gather(jnp.concatenate(spectra, 0), "chan", axis=0, tiled=False)
    left = arrange(gathered)
    half = stack(left, first, 0, None)
    return stack(left, second, 1, half)


def solution(mesh):
    return jax.shard_map(
        shards,
        mesh=mesh,
        in_specs=(P("tm", "chan", None), P(), P()),
        out_specs=P("tm", None, None, "chan"),
        check_vma=False,
    )
```

time: 708 us -> 200 us (0.28)
  waiting for transfers between devices: 490 us -> 77.1 us
  local copies, waits for them, and re-layouts: 109 us -> 10.9 us
  Pallas kernels: 0 us -> 59.1 us
  matrix products: 42.3 us -> 0 us
  other arithmetic: 37.4 us -> 21.7 us
    psum x1 -> x0, waiting for transfers between devices: 356 us -> none  [shards(): source = lax.psum(partial_value.astype(jnp.bfloat16), 'chan')]
    all_to_all x2 -> x1, waiting for transfers between devices: 134 us -> 26.1 us  [shards(): lax.all_to_all(encode(samples, source_index), 'chan', 0, 0, tiled=True)]
    unnamed x9 -> x18, local copies, waits for them, and re-layouts: 79.9 us -> 1.97 us
    pallas_call x0 -> x7, Pallas kernels: none -> 59.1 us  [the longest x2 18.6 us: transform(): pl.pallas_call(transform_kernel, grid_spec=pltpu.PrefetchScalarGridSpec(n...]
    all_gather x0 -> x1, waiting for transfers between devices: none -> 48.4 us  [shards(): lax.all_gather(jnp.concatenate(spectra, 0), 'chan', axis=0, tiled=False)]
    dot_general x3 -> x0, matrix products: 42.3 us -> none  [the longest x1 24.3 us: transform(): jnp.einsum('kwc,wg->kgc', blocks, dft_rows, precision=lax.Precision.HIGHE...]
    all_to_all x3 -> x0, local copies, waits for them, and re-layouts: 22.5 us -> none  [the longest x2 20 us: shards(): lax.all_to_all(samples, 'chan', split_axis=2, concat_axis=1, tiled=True)]
    all_to_all x1 -> x0, other arithmetic: 19.4 us -> none  [shards(): lax.all_to_all(samples, 'chan', split_axis=2, concat_axis=1, tiled=True)]
  transfers between devices with their start and end apart: 3 -> 11, of which waited for: 3 -> 4; matrix products, arithmetic and copies ran while one was open for 1% -> 11% of each run, Pallas kernels for 0% -> 18%
where the time goes in v1:
time: 200 us; the launch traced here: 199 us
  waiting for transfers between devices  77.1 us (39%)
  Pallas kernels  59.1 us (30%)
  other arithmetic  21.7 us (11%)
  starting transfers between devices  16.5 us (8%)
  between operations  13.6 us (7%)
  local copies, waits for them, and re-layouts  10.9 us (5%)
    all_gather x1, waiting for transfers between devices, shards(): lax.all_gather(jnp.concatenate(spectra, 0), 'chan', axis=0, tiled=False)  48.4 us
    all_to_all x1, waiting for transfers between devices, shards(): lax.all_to_all(encode(samples, source_index), 'chan', 0, 0, tiled=True)  26.1 us
    pallas_call x2, Pallas kernels, transform(): pl.pallas_call(transform_kernel, grid_spec=pltpu.PrefetchScalarGridSpec(n...  18.6 us
    pallas_call x2, Pallas kernels, stack(): pl.pallas_call(stack_kernel, grid=(steps,), in_specs=[pl.BlockSpec((2, 2...  16.7 us
    mul x1, other arithmetic, dft_table(): table = taper * jnp.cos(phase.astype(f32) * (2.0 * math.pi / WIN))  15.8 us
    all_to_all x1, starting transfers between devices, shards(): lax.all_to_all(encode(samples, source_index), 'chan', 0, 0, tiled=True)  10.8 us
    pallas_call x1, Pallas kernels, encode(): pl.pallas_call(encode_kernel, grid=(samples.shape[2] // wide,), in_specs=...  9.77 us
    pallas_call x1, Pallas kernels, arrange(): pl.pallas_call(arrange_kernel, in_specs=[whole], out_specs=whole, out_sha...  9.08 us
  transfers between devices with their start and end apart: 11, of which 4 were waited for; matrix products, arithmetic and copies ran while one was open for 11% of the time, Pallas kernels for 18%

profile of v1, /device:TPU:0, one launch (start us, length us, event | category | flops | bytes accessed | tf_op | source)
XLA Modules:
  0.0 198.8 jit_solution(1698087609064034210)
XLA Ops:
  6.5 1.4 copy.13.source
  7.9 9.8 %encode.1 = s16[32,208,256]{2,1,0:T(8,128)(2,1)} custom-call(f32[6,32,8192]{2,1,0:T(8,128)} %samples.1, s32[128,1]{1,0:T(8,128)} %copy.13.source), custom_call_target="tpu_custom_call" | custom-call | tf_op jit(solution)/shard_map/encode/pallas_call | solution.py:109
  17.7 10.8 %all-to-all-start = ((s16[32,208,256]{2,1,0:T(8,128)(2,1)}), s16[32,208,256]{2,1,0:T(8,128)(2,1)S(1)}, u32[]{:S(2)}, u32[]{:S(2)}) async-start(s16[32,208,256]{2,1,0:T(8,128)(2,1)} %encode.1), calls=%async_computation | async-start | bytes 6815744 | tf_op jit(solution)/shard_map/all_to_all | solution.py:318
  28.5 0.0 all-gather.3.cloned.1.call-start
  28.6 0.1 reshape.153
  28.7 0.2 fusion.21
  28.9 0.6 gather_fusion
  29.5 0.7 reshape_tile.4.live
  30.3 15.8 %fusion.5 = f32[1024,1024]{1,0:T(8,128)S(1)} fusion(s32[1024]{0:T(1024)S(1)} %get-tuple-element.32, s32[1024]{0:T(1024)S(1)} %get-tuple-element.31, f32[1024]{0:T(1024)S(1)} %multiply_subtract_fusion), kind=kLoop, calls=%fused_computation.11 | loop fusion | flops 16777216 | bytes 4206592 | tf_op jit(solution)/shard_map/mul | solution.py:46
  46.1 2.9 %fusion = (bf16[1024,1024]{1,0:T(8,128)(2,1)}, bf16[1024,1024]{1,0:T(8,128)(2,1)}) fusion(f32[1024,1024]{1,0:T(8,128)S(1)} %fusion.5), kind=kLoop, calls=%fused_computation.6 | loop fusion | flops 4194304 | bytes 8388608 | tf_op jit(solution)/shard_map/convert_element_type | solution.py:49
  49.0 26.1 %all-to-all-done.codes.extra = s16[32,208,256]{2,1,0:T(8,128)(2,1)S(1)} async-done(((s16[32,208,256]{2,1,0:T(8,128)(2,1)}), s16[32,208,256]{2,1,0:T(8,128)(2,1)S(1)}, u32[]{:S(2)}, u32[]{:S(2)}) %all-to-all-start) | async-done | bytes 3407904 | tf_op jit(solution)/shard_map/all_to_all | solution.py:318
  75.1 0.1 fusion.7
  75.3 0.8 copy.14
  76.1 2.0 %reshape.151 = f32[32,4,6,32]{3,2,0,1:T(8,128)} reshape(f32[32,4,192]{2,0,1:T(8,128)} %copy.14) | data formatting | bytes 196608 | tf_op jit(solution)/shard_map/reshape | solution.py:206
  78.1 1.2 multiply_bitcast_fusion
  79.4 0.8 copy.17
  80.2 1.8 reshape.152.x
  82.0 5.0 %sources.1 = (bf16[24,256]{1,0:T(8,128)(2,1)}, bf16[24,256]{1,0:T(8,128)(2,1)}, bf16[24,256]{1,0:T(8,128)(2,1)}, bf16[24,256]{1,0:T(8,128)(2,1)}) custom-call(s32[1]{0:T(128)} %bitcast.mine, f32[24,1024]{1,0:T(8,128)} %reshape.152.x, bf16[1024,1024]{1,0:T(8,128)(2,1)} %get-tuple-element.30.high, bf16[1024,1024]{1,0:T(8,128)(2,1)} %get-tuple-element.29.low, ...), custom_call_target="tpu_custom_call" | custom-call | tf_op jit(solution)/shard_map/sources/pallas_call | solution.py:211
  87.0 0.0 collective-permute-start
  87.0 1.0 collective-permute-start.1
  88.0 0.8 collective-permute-start.2
  88.8 0.0 collective-permute-done
  88.8 2.1 %collective-permute-done.1 = bf16[24,256]{1,0:T(8,128)(2,1)S(1)} collective-permute-done((bf16[24,256]{1,0:T(8,128)(2,1)}, bf16[24,256]{1,0:T(8,128)(2,1)S(1)}, u32[]{:S(2)}, u32[]{:S(2)}) %collective-permute-start.1) | collective-permute-done | bytes 12320 | tf_op jit(solution)/shard_map/ppermute | solution.py:305
  90.9 0.4 collective-permute-done.2
  91.3 1.3 pad_maximum_fusion
  92.7 0.0 all-gather.3.cloned.1.call-update
  92.7 0.7 dynamic_slice.7
  93.3 9.3 %transform.3 = (bf16[6,128,256]{2,1,0:T(8,128)(2,1)}, bf16[6,128,256]{2,1,0:T(8,128)(2,1)}, bf16[6,128,256]{2,1,0:T(8,128)(2,1)}, bf16[6,128,256]{2,1,0:T(8,128)(2,1)}) custom-call(s32[1]{0:T(128)} %bitcast.mine, s16[32,208,256]{2,1,0:T(8,128)(2,1)} %copy-done, s16[32,208,256]{2,1,0:T(8,128)(2,1)} %copy-done, bf16[4,2,128,1024]{3,2,1,0:T(8,128)(2,1)} %bitcast.15, ...), custom_call_target="tpu_custom_call" | custom-call | tf_op jit(solution)/shard_map/transform/pallas_call | solution.py:154
  102.7 0.2 collective-permute-start.6
  102.9 1.0 collective-permute-start.7
  103.9 0.6 collective-permute-start.8
  104.5 9.3 %transform.2 = (bf16[6,128,256]{2,1,0:T(8,128)(2,1)}, bf16[6,128,256]{2,1,0:T(8,128)(2,1)}, bf16[6,128,256]{2,1,0:T(8,128)(2,1)}, bf16[6,128,256]{2,1,0:T(8,128)(2,1)}) custom-call(s32[1]{0:T(128)} %bitcast.mine, s16[32,208,256]{2,1,0:T(8,128)(2,1)} %copy-done, s16[32,208,256]{2,1,0:T(8,128)(2,1)} %copy-done, bf16[4,2,128,1024]{3,2,1,0:T(8,128)(2,1)} %bitcast.16, ...), custom_call_target="tpu_custom_call" | custom-call | tf_op jit(solution)/shard_map/transform/pallas_call | solution.py:154
  113.8 0.5 collective-permute-start.3
  114.3 1.0 collective-permute-start.4
  115.3 0.0 collective-permute-done.6.b
  115.3 0.4 collective-permute-start.5
  115.8 48.4 %all-gather.3.cloned.1.call-done = bf16[3072,256]{1,0:T(8,128)(2,1)} async-done(((bf16[96,256]{1,0:T(8,128)(2,1)}), bf16[3072,256]{1,0:T(8,128)(2,1)}) %all-gather.3.cloned.1.call-update) | async-done | bytes 1572880 | tf_op jit(solution)/shard_map/all_gather | solution.py:322
  164.2 9.1 %arrange.1.left = bf16[32,256,192]{2,1,0:T(8,128)(2,1)} custom-call(bf16[32,96,256]{2,1,0:T(8,128)(2,1)} %bitcast.17), custom_call_target="tpu_custom_call" | custom-call | tf_op jit(solution)/shard_map/arrange/pallas_call | solution.py:254
  173.3 0.0 collective-permute-done.7.c
  173.3 0.8 copy-done.5
  174.1 0.2 copy-done.6
  174.2 8.3 %stack.2.rest_0_ = bf16[128,2,128,256]{3,2,1,0:T(8,128)(2,1)} custom-call(bf16[32,256,192]{2,1,0:T(8,128)(2,1)} %arrange.1.left, bf16[6,128,256]{2,1,0:T(8,128)(2,1)} %get-tuple-element.25.a, bf16[6,128,256]{2,1,0:T(8,128)(2,1)} %copy-done.4, bf16[6,128,256]{2,1,0:T(8,128)(2,1)} %copy-done.5, bf16[6,128,256]{2,1,0:T(8,128)(2,1)} %copy-done.6), custom_call_target="tpu_custom_call" | custom-call | tf_op jit(solution)/shard_map/stack/pallas_call | solution.py:288
  182.5 0.0 collective-permute-done.3.b
  182.6 0.0 collective-permute-done.4.c
  182.6 0.7 copy-done.1
  183.3 0.1 copy-done.2
  183.4 0.2 copy-done.3
  183.6 8.3 %stack.3 = bf16[128,2,128,256]{3,2,1,0:T(8,128)(2,1)} custom-call(bf16[32,256,192]{2,1,0:T(8,128)(2,1)} %arrange.1.left, bf16[6,128,256]{2,1,0:T(8,128)(2,1)} %get-tuple-element.21.a, bf16[6,128,256]{2,1,0:T(8,128)(2,1)} %copy-done.1, bf16[6,128,256]{2,1,0:T(8,128)(2,1)} %copy-done.2, ...), custom_call_target="tpu_custom_call", output_to_operand_aliasing={{}: (5, {})} | custom-call | tf_op jit(solution)/shard_map/stack/pallas_call | solution.py:288
  (22 shorter events, 0.1 us)
Async XLA Ops:
  17.7 10.9 %copy-start.8 = (s32[128]{0:T(128)S(1)}, s32[128]{0:T(128)}, u32[]{:S(2)}) copy-start(s32[128]{0:T(128)} %param.4) | copy-start | bytes 1540
  17.7 11.2 %copy-start.7 = (s32[8192]{0:T(1024)S(1)}, s32[8192]{0:T(1024)}, u32[]{:S(2)}) copy-start(s32[8192]{0:T(1024)} %param.5) | copy-start | bytes 98308
  17.7 57.4 %all-to-all-start = ((s16[32,208,256]{2,1,0:T(8,128)(2,1)}), s16[32,208,256]{2,1,0:T(8,128)(2,1)S(1)}, u32[]{:S(2)}, u32[]{:S(2)}) async-start(s16[32,208,256]{2,1,0:T(8,128)(2,1)} %encode.1), calls=%async_computation | async-start | bytes 6815744 | tf_op jit(solution)/shard_map/all_to_all | solution.py:318
  28.5 135.6 %all-gather.3.cloned.1.call-start = ((), (), s32[]{:S(2)}) async-start(), calls=%async_computation.1 | async-start | bytes 1622016 | tf_op jit(solution)/shard_map/all_gather | solution.py:322
  75.1 18.3 %copy-start = (s16[32,208,256]{2,1,0:T(8,128)(2,1)}, s16[32,208,256]{2,1,0:T(8,128)(2,1)S(1)}, u32[]{:S(2)}) copy-start(s16[32,208,256]{2,1,0:T(8,128)(2,1)S(1)} %all-to-all-done.codes.extra) | copy-start | bytes 10223620
  87.0 1.9 collective-permute-start
  87.0 3.9 %collective-permute-start.1 = (bf16[24,256]{1,0:T(8,128)(2,1)}, bf16[24,256]{1,0:T(8,128)(2,1)S(1)}, u32[]{:S(2)}, u32[]{:S(2)}) collective-permute-start(bf16[24,256]{1,0:T(8,128)(2,1)} %get-tuple-element.19), channel_id=1, source_target_pairs={{0,64},{32,96},{64,0},{96,32},{1,65},{33,97},{65,1},{97,33},{2,66}... | collective-permute-start | bytes 36872 | tf_op jit(solution)/shard_map/ppermute | solution.py:305
  88.0 3.3 %collective-permute-start.2 = (bf16[24,256]{1,0:T(8,128)(2,1)}, bf16[24,256]{1,0:T(8,128)(2,1)S(1)}, u32[]{:S(2)}, u32[]{:S(2)}) collective-permute-start(bf16[24,256]{1,0:T(8,128)(2,1)} %get-tuple-element.20), channel_id=1, source_target_pairs={{0,96},{32,64},{64,32},{96,0},{1,97},{33,65},{65,33},{97,1},{2,98}... | collective-permute-start | bytes 36872 | tf_op jit(solution)/shard_map/ppermute | solution.py:305
  102.7 12.7 %collective-permute-start.6 = (bf16[6,128,256]{2,1,0:T(8,128)(2,1)}, bf16[6,128,256]{2,1,0:T(8,128)(2,1)S(1)}, u32[]{:S(2)}, u32[]{:S(2)}) collective-permute-start(bf16[6,128,256]{2,1,0:T(8,128)(2,1)} %get-tuple-element.26), channel_id=1, source_target_pairs={{0,32},{32,0},{64,96},{96,64},{1,33},{33,1},{65,97},{97,65},{2,34}... | collective-permute-start | bytes 1179656 | tf_op jit(solution)/shard_map/ppermute | solution.py:305
  102.9 70.4 %collective-permute-start.7 = (bf16[6,128,256]{2,1,0:T(8,128)(2,1)}, bf16[6,128,256]{2,1,0:T(8,128)(2,1)S(1)}, u32[]{:S(2)}, u32[]{:S(2)}) collective-permute-start(bf16[6,128,256]{2,1,0:T(8,128)(2,1)} %get-tuple-element.27), channel_id=1, source_target_pairs={{0,64},{32,96},{64,0},{96,32},{1,65},{33,97},{65,1},{97,33},{2,66}... | collective-permute-start | bytes 1179656 | tf_op jit(solution)/shard_map/ppermute | solution.py:305
  103.9 69.4 %collective-permute-start.8 = (bf16[6,128,256]{2,1,0:T(8,128)(2,1)}, bf16[6,128,256]{2,1,0:T(8,128)(2,1)S(1)}, u32[]{:S(2)}, u32[]{:S(2)}) collective-permute-start(bf16[6,128,256]{2,1,0:T(8,128)(2,1)} %get-tuple-element.28), channel_id=1, source_target_pairs={{0,96},{32,64},{64,32},{96,0},{1,97},{33,65},{65,33},{97,1},{2,98}... | collective-permute-start | bytes 1179656 | tf_op jit(solution)/shard_map/ppermute | solution.py:305
  113.8 68.7 %collective-permute-start.3 = (bf16[6,128,256]{2,1,0:T(8,128)(2,1)}, bf16[6,128,256]{2,1,0:T(8,128)(2,1)S(1)}, u32[]{:S(2)}, u32[]{:S(2)}) collective-permute-start(bf16[6,128,256]{2,1,0:T(8,128)(2,1)} %get-tuple-element.22), channel_id=1, source_target_pairs={{0,32},{32,0},{64,96},{96,64},{1,33},{33,1},{65,97},{97,65},{2,34}... | collective-permute-start | bytes 1179656 | tf_op jit(solution)/shard_map/ppermute | solution.py:305
  114.3 68.3 %collective-permute-start.4 = (bf16[6,128,256]{2,1,0:T(8,128)(2,1)}, bf16[6,128,256]{2,1,0:T(8,128)(2,1)S(1)}, u32[]{:S(2)}, u32[]{:S(2)}) collective-permute-start(bf16[6,128,256]{2,1,0:T(8,128)(2,1)} %get-tuple-element.23), channel_id=1, source_target_pairs={{0,64},{32,96},{64,0},{96,32},{1,65},{33,97},{65,1},{97,33},{2,66}... | collective-permute-start | bytes 1179656 | tf_op jit(solution)/shard_map/ppermute | solution.py:305
  115.3 58.0 %copy-start.4 = (bf16[6,128,256]{2,1,0:T(8,128)(2,1)}, bf16[6,128,256]{2,1,0:T(8,128)(2,1)S(1)}, u32[]{:S(2)}) copy-start(bf16[6,128,256]{2,1,0:T(8,128)(2,1)S(1)} %collective-permute-done.6.b) | copy-start | bytes 1179652
  115.3 67.2 %collective-permute-start.5 = (bf16[6,128,256]{2,1,0:T(8,128)(2,1)}, bf16[6,128,256]{2,1,0:T(8,128)(2,1)S(1)}, u32[]{:S(2)}, u32[]{:S(2)}) collective-permute-start(bf16[6,128,256]{2,1,0:T(8,128)(2,1)} %get-tuple-element.24), channel_id=1, source_target_pairs={{0,96},{32,64},{64,32},{96,0},{1,97},{33,65},{65,33},{97,1},{2,98}... | collective-permute-start | bytes 1179656 | tf_op jit(solution)/shard_map/ppermute | solution.py:305
  173.3 0.8 copy-start.5
  173.3 0.9 copy-start.6
  182.6 0.7 copy-start.1
  182.6 0.9 copy-start.2
  182.6 1.0 copy-start.3
Sparse Core Ops, SparseCore 0:
  92.8 71.3 all-gather.2

commit v2 on v0

v2 whole, which is shorter than its diff:
```python
import functools
import math

import jax
import jax.numpy as jnp
from jax import lax
from jax.experimental import pallas as pl
from jax.experimental.pallas import tpu as pltpu
from jax.sharding import PartitionSpec as P

WIN = 1024
BINS = 512
BAND = 64
WINDOWS = 24
SOURCES = 128
CHAN = 32
TM = 4
KW = WINDOWS // TM
SUB = WIN // CHAN
WIDTH = 256
NEAR = 16
PICK = SOURCES // NEAR
DATA = KW * SUB
ROWS = DATA + 16
GROUP = 4
DEPTH = WINDOWS * 2 * GROUP
STEPS = 128.0
TOP = 32767.0
ROUND = 1.5 * 2.0**23
EPS = 1e-06
VMEM = 56 * 1024 * 1024

f32 = jnp.float32
bf16 = jnp.bfloat16


def split(x):
    high = x.astype(bf16)
    return high, (x - high.astype(f32)).astype(bf16)


def dft_table():
    row = jnp.arange(2 * BINS, dtype=jnp.int32)[:, None]
    sample = jnp.arange(WIN, dtype=jnp.int32)[None, :]
    rows = 2 * BAND
    place = row // (TM * rows) * BAND + row // rows % TM * (2 * BAND)
    frequency = place + row % rows // (2 * GROUP) * GROUP + row % GROUP
    part = row // GROUP % 2
    phase = (sample * frequency + part * (WIN // 4)) % WIN
    taper = 0.5 - 0.5 * jnp.cos((sample.astype(f32) + 0.5) * (2.0 * math.pi / WIN))
    table = taper * jnp.cos(phase.astype(f32) * (2.0 * math.pi / WIN))
    table = lax.optimization_barrier(table).reshape(2, BINS, WIN)
    high = lax.reduce_precision(table, 8, 7)
    return jnp.concatenate([high.astype(bf16), (table - high).astype(bf16)], 1)


def scale_of(code):
    return jnp.exp2(code * (1.0 / STEPS)) * (1.0 / TOP)


def encode_kernel(samples, source, result, out, picked, extra, sems):
    step = pl.program_id(0)
    wide = samples.shape[2]
    blocks = wide // WIDTH
    steps = CHAN // blocks

    def copy(i):
        here = pl.ds(i * blocks, blocks)
        return pltpu.make_async_copy(
            out.at[here, :DATA, :], result.at[here, :DATA, :], sems.at[i]
        )

    @pl.when(step == 0)
    def _():
        picked[...] = jnp.zeros_like(picked)
        extra[...] = jnp.zeros_like(extra)

    number = lax.broadcasted_iota(jnp.int32, (wide, SOURCES), 0) + step * wide
    chooser = jnp.where(source[...] == number, 1.0, 0.0).astype(bf16)
    codes = []
    scales = []
    for w in range(KW):
        x = samples[w]
        peak = jnp.max(jnp.abs(x), axis=0, keepdims=True)
        scale = jnp.ceil(jnp.log2(jnp.maximum(peak, 1e-30)) * STEPS) + 1.0
        q = (x * (jnp.exp2(scale * (-1.0 / STEPS)) * TOP) + ROUND) - ROUND
        codes.append(q)
        scales.append(scale)
        qi = q.astype(jnp.int32).astype(jnp.int16)
        for k in range(blocks):
            out[step * blocks + k, w * SUB : (w + 1) * SUB, :] = qi[:, k * WIDTH : (k + 1) * WIDTH]
    copy(step).start()
    scales = jnp.concatenate(scales + [jnp.zeros((16 - KW, wide), f32)], 0)
    for k in range(blocks):
        for half in range(2):
            lane = k * WIDTH + half * 128
            start = pl.multiple_of((step * blocks + k) * 16 + 8, 8)
            extra[half, pl.ds(start, 8), :] = scales[:8, lane : lane + 128]
    high, low = split(jnp.concatenate(codes + [scales], 0))
    both = jnp.dot(jnp.concatenate([high, low], 0), chooser, preferred_element_type=f32)
    picked[:ROWS, :] += both[:ROWS] + both[ROWS:]

    @pl.when(step == pl.num_programs(0) - 1)
    def _():
        chosen = picked[...].T
        for half in range(2):
            part = chosen[:, half * 128 : half * 128 + 128]
            for d in range(NEAR):
                for z in range(2):
                    row = (d // 4 * 8 + z * 4 + d % 4) * 16
                    extra[half, row : row + PICK, :] = part[d * PICK : (d + 1) * PICK]
            rows = extra[half].reshape(CHAN, 16, 128)
            out[:, DATA:, half * 128 : half * 128 + 128] = rows.astype(jnp.int32).astype(jnp.int16)
        last = pltpu.make_async_copy(out.at[:, DATA:, :], result.at[:, DATA:, :], sems.at[steps])
        last.start()
        for i in range(steps):
            copy(i).wait()
        last.wait()


def encode(samples, source_index):
    wide = 2048
    steps = samples.shape[2] // wide
    return pl.pallas_call(
        encode_kernel,
        grid=(steps,),
        in_specs=[
            pl.BlockSpec((KW, SUB, wide), lambda i: (0, 0, i)),
            pl.BlockSpec((1, SOURCES), lambda i: (0, 0)),
        ],
        out_specs=pl.BlockSpec(memory_space=pl.ANY),
        out_shape=jax.ShapeDtypeStruct((CHAN, ROWS, WIDTH), jnp.int16),
        scratch_shapes=[
            pltpu.VMEM((CHAN, ROWS, WIDTH), jnp.int16),
            pltpu.VMEM((WIDTH, SOURCES), f32),
            pltpu.VMEM((2, CHAN * 16, 128), f32),
            pltpu.SemaphoreType.DMA((steps + 1,)),
        ],
        compiler_params=pltpu.CompilerParams(vmem_limit_bytes=VMEM),
        name="encode",
    )(samples, source_index.reshape(1, SOURCES))


def transform_kernel(mine, codes, extra, table, live, *rest):
    outs, (scale, white) = rest[:-2], rest[-2:]
    step = pl.program_id(0)
    rows = 2 * BAND
    batch = codes.shape[1] // SUB

    @pl.when(step == 0)
    def _():
        scale[...] = scale_of(extra[...].astype(jnp.int32).astype(f32)[:, 8:, :])

    for v in range(batch):
        value = codes[:, v * SUB : (v + 1) * SUB, :].astype(jnp.int32).astype(f32)
        value = value * scale[:, pl.ds(step * batch + v, 1), :]
        high, low = split(value.reshape(WIN, WIDTH))
        y = jnp.dot(table[0], high, preferred_element_type=f32)
        z = jnp.dot(table[0, : TM * rows], low, preferred_element_type=f32)
        for k in range(TM):
            part = slice(k * rows, (k + 1) * rows)
            value = y[part] + (y[(TM + k) * rows : (TM + k + 1) * rows] + z[part])
            power = jnp.sum(value * value, axis=0, keepdims=True) * (1.0 / BAND)
            white[k] = (value * (live[...] * lax.rsqrt(power + EPS))).astype(bf16)
        for k in range(TM):
            outs[k][v * rows : (v + 1) * rows, :] = white[jnp.bitwise_xor(mine[0], k)]


def transform(mine, received, table, live, band):
    rows = 2 * BAND
    batch = 2
    piece = pl.BlockSpec((batch * rows, WIDTH), lambda w, _: (w, 0))
    out_specs = [piece] * TM
    shapes = [jax.ShapeDtypeStruct((KW * rows, WIDTH), bf16)] * TM
    return pl.pallas_call(
        transform_kernel,
        grid_spec=pltpu.PrefetchScalarGridSpec(
            num_scalar_prefetch=1,
            grid=(KW // batch,),
            in_specs=[
                pl.BlockSpec((CHAN, batch * SUB, WIDTH), lambda w, _: (0, w, 0)),
                pl.BlockSpec((CHAN, 16, WIDTH), lambda w, _: (0, DATA // 16, 0)),
                pl.BlockSpec((1, 2 * BINS, WIN), lambda w, _: (band, 0, 0)),
                pl.BlockSpec((1, WIDTH), lambda w, _: (0, 0)),
            ],
            out_specs=out_specs,
            scratch_shapes=[pltpu.VMEM((CHAN, 8, WIDTH), f32), pltpu.VMEM((TM, rows, WIDTH), bf16)],
        ),
        out_shape=shapes,
        compiler_params=pltpu.CompilerParams(vmem_limit_bytes=VMEM),
        cost_estimate=pl.CostEstimate(flops=40 * 10**9, bytes_accessed=10**8, transcendentals=0),
        name="transform",
    )(mine, received, received, table, live)


def sources_kernel(mine, extra, table, live, *rest):
    outs, (x, bands) = rest[:TM], rest[TM:]
    for first in range(0, CHAN, 4):
        values = [extra[d].astype(jnp.int32).astype(f32)[:PICK] for d in range(first, first + 4)]
        scales = [scale_of(value[:, DATA : DATA + KW]) for value in values]
        for w in range(KW):
            x[w * PICK : (w + 1) * PICK, first * SUB : (first + 4) * SUB] = jnp.concatenate(
                [
                    value[:, w * SUB : (w + 1) * SUB] * scale[:, w : w + 1]
                    for value, scale in zip(values, scales)
                ],
                1,
            )
    high, low = split(x[...])
    over = (((1,), (1,)), ((), ()))
    rows = 2 * BAND
    for b in range(2):
        y = lax.dot_general(high, table[b], over, preferred_element_type=f32)
        z = lax.dot_general(low, table[b, : TM * rows], over, preferred_element_type=f32)
        value = y[:, : TM * rows] + (y[:, TM * rows :] + z)
        for k in range(TM):
            band = value[:, k * rows : (k + 1) * rows]
            power = jnp.sum(band * band, axis=1, keepdims=True) * (1.0 / BAND)
            bands[b, k] = band * (live[...] * lax.rsqrt(power + EPS))
    for b in range(2):
        for k in range(TM):
            value = bands[b, jnp.bitwise_xor(mine[0], k)]
            outs[k][:, b * rows : (b + 1) * rows] = value.astype(bf16)


def sources(mine, received, table, live):
    rows = 2 * BAND
    piece = pl.BlockSpec((KW * PICK, WIDTH), lambda i: (0, 0))
    return pl.pallas_call(
        sources_kernel,
        grid=(1,),
        in_specs=[
            pl.BlockSpec(memory_space=pltpu.SMEM),
            pl.BlockSpec((CHAN, 16, WIDTH), lambda i: (0, DATA // 16, 0)),
            pl.BlockSpec((2, 2 * BINS, WIN), lambda i: (0, 0, 0)),
            pl.BlockSpec((KW * PICK, 1), lambda i: (0, 0)),
        ],
        out_specs=[piece] * TM,
        out_shape=[jax.ShapeDtypeStruct((KW * PICK, WIDTH), bf16)] * TM,
        scratch_shapes=[pltpu.VMEM((KW * PICK, WIN), f32), pltpu.VMEM((2, TM, KW * PICK, rows), f32)],
        compiler_params=pltpu.CompilerParams(vmem_limit_bytes=VMEM),
        name="sources",
    )(mine, received, table, live)


def pack_kernel(a, b, c, d, out):
    parts = [u[...].astype(f32) for u in (a, b, c, d)]
    rows = [part[w * PICK : (w + 1) * PICK] for part in parts for w in range(KW)]
    block = lax.broadcasted_iota(jnp.int32, (PICK, 128), 1) // (2 * GROUP)
    for band in range(2):
        tiles = []
        pieces = [row[:, band * 128 : band * 128 + 128] for row in rows]
        for g in range(16):
            tile = jnp.zeros((PICK, 128), f32)
            for v in range(16):
                tile = jnp.where(block == v, pltpu.roll(pieces[v], (v - g) * 8 % 128, 1), tile)
            tiles.append(tile)
        for g in range(8):
            tile = jnp.zeros((PICK, 128), f32)
            for v in range(16):
                shift = (v - g * 2 - v // 8) * 8 % 128
                tile = jnp.where(block == v, pltpu.roll(pieces[16 + v % 8], shift, 1), tile)
            tiles.append(tile)
        value = jnp.concatenate(tiles, 0).astype(bf16)
        for d in range(NEAR):
            out[d, band] = value


def pack(spectra):
    whole = pl.BlockSpec(memory_space=pltpu.VMEM)
    return pl.pallas_call(
        pack_kernel,
        in_specs=[whole] * TM,
        out_specs=whole,
        out_shape=jax.ShapeDtypeStruct((NEAR, 2, 24 * PICK, 128), bf16),
        compiler_params=pltpu.CompilerParams(vmem_limit_bytes=VMEM),
        name="pack",
    )(*spectra)


def stack_kernel(band, sources, a, b, c, d, *rest):
    result, out, tiles, sems = rest[-4:]
    steps = BAND // GROUP // 2
    column = lax.broadcasted_iota(jnp.int32, (1, DEPTH), 1) % GROUP
    masks = [jnp.where(column == i, 1.0, 0.0).astype(bf16) for i in range(GROUP)]
    second = lax.broadcasted_iota(jnp.int32, (1, 128), 1) // GROUP % 2 == 1

    def copy(g):
        start = band * BAND + g * 2 * GROUP
        return pltpu.make_async_copy(
            out.at[pl.ds(g * 2 * GROUP, 2 * GROUP)],
            result.at[pl.ds(start, 2 * GROUP)],
            sems.at[g],
        )

    for place in range(NEAR):
        value = sources[place, 0].astype(f32).reshape(24, PICK, 128)
        tiles[:, place * PICK : (place + 1) * PICK, :] = value

    def imaginary(value):
        ahead = pltpu.roll(value, 128 - GROUP, 1)
        behind = pltpu.roll(value, GROUP, 1)
        return jnp.where(second, -behind, ahead)

    def body(g, carry):
        parts = [
            jnp.stack([u[pl.ds(pl.multiple_of(w * 2 * BAND + g * 16, 16), 16), :] for w in range(KW)])
            for u in (a, b, c, d)
        ]
        parts = [u.astype(f32) for u in parts]
        late = tiles[16 + g]
        for h in range(2):
            right = jnp.concatenate([u[:, h * 8 : h * 8 + 8, :] for u in parts], 0)
            right = right.reshape(DEPTH, WIDTH).astype(bf16)
            early = tiles[g * 2 + h]
            later = pltpu.roll(late, 64, 1) if h else late
            value = jnp.concatenate(
                [
                    jnp.concatenate([early, imaginary(early)], 0),
                    jnp.concatenate([later, imaginary(later)], 0)[:, :64],
                ],
                1,
            ).astype(bf16)
            for i in range(GROUP):
                product = jnp.dot(value * masks[i], right, preferred_element_type=f32)
                out[(g * 2 + h) * GROUP + i] = (
                    (product * (1.0 / WINDOWS)).reshape(2, SOURCES, WIDTH).astype(bf16)
                )
        copy(g).start()
        return carry

    lax.fori_loop(0, steps, body, 0)

    def finish(g, carry):
        copy(g).wait()
        return carry

    lax.fori_loop(0, steps, finish, 0)


def stack(sources, parts, band, before):
    whole = pl.BlockSpec((KW * 2 * BAND, WIDTH), lambda i: (0, 0))
    extra = [] if before is None else [before]
    return pl.pallas_call(
        functools.partial(stack_kernel, band),
        grid=(1,),
        in_specs=[pl.BlockSpec((NEAR, 1, 24 * PICK, 128), lambda i: (0, band, 0, 0))]
        + [whole] * TM
        + [pl.BlockSpec(memory_space=pl.ANY)] * len(extra),
        out_specs=pl.BlockSpec(memory_space=pl.ANY),
        out_shape=jax.ShapeDtypeStruct((BINS // TM, 2, SOURCES, WIDTH), bf16),
        scratch_shapes=[
            pltpu.VMEM((BAND, 2, SOURCES, WIDTH), bf16),
            pltpu.VMEM((24, SOURCES, 128), f32),
            pltpu.SemaphoreType.DMA((BAND // GROUP // 2,)),
        ],
        input_output_aliases={} if before is None else {1 + TM: 0},
        compiler_params=pltpu.CompilerParams(vmem_limit_bytes=VMEM),
        name="stack",
    )(sources, *parts, *extra)


def swap(value, axis, size, distance):
    return lax.ppermute(value, axis, [(i, i ^ distance) for i in range(size)])


def after(value, *others):
    return lax.optimization_barrier((value,) + others)[0]


def shards(samples, source_index, dead_flags):
    place = lax.axis_index("chan").astype(jnp.int32)
    mine = lax.axis_index("tm").astype(jnp.int32).reshape(1)
    live_all = 1.0 - dead_flags.astype(f32)
    live = lax.dynamic_slice_in_dim(live_all, place * WIDTH, WIDTH).reshape(1, WIDTH)
    place = place // 8 * 4 + place % 4
    own_sources = lax.dynamic_slice_in_dim(source_index, place * PICK, PICK)
    live_source = jnp.tile(live_all[own_sources], KW).reshape(KW * PICK, 1)
    table = dft_table()

    received = lax.all_to_all(encode(samples, source_index), "chan", 0, 0, tiled=True)
    spectra = sources(mine, received, table, live_source)
    spectra = [spectra[0]] + [swap(spectra[k], "tm", TM, k) for k in range(1, TM)]
    pieces = transform(mine, after(received, spectra[0]), table, live, 0)
    first = [pieces[0]] + [swap(after(pieces[k], *spectra[1:]), "tm", TM, k) for k in range(1, TM)]
    packed = pack([after(spectra[0], pieces[0])] + spectra[1:])
    groups = [[x * 8 + z * 4 + y for x in range(4) for y in range(4)] for z in range(2)]
    left = lax.all_to_all(packed, "chan", 0, 0, tiled=True, axis_index_groups=groups)
    pieces = transform(mine, after(received, packed), table, live, 1)
    second = [pieces[0]] + [
        swap(after(pieces[k], *first[2:]), "tm", TM, k) for k in range(1, TM)
    ]
    result = stack(left, first, 0, None)
    return stack(left, second, 1, result)


def solution(mesh):
    return jax.shard_map(
        shards,
        mesh=mesh,
        in_specs=(P("tm", "chan", None), P(), P()),
        out_specs=P("tm", None, None, "chan"),
        check_vma=False,
    )
```

time: 708 us -> 135 us (0.19)
  waiting for transfers between devices: 490 us -> 37.8 us
  local copies, waits for them, and re-layouts: 109 us -> 6.66 us
  Pallas kernels: 0 us -> 46.2 us
  matrix products: 42.3 us -> 0 us
  other arithmetic: 37.4 us -> 19.3 us
  between operations: 13.5 us -> 0.4 us
  starting transfers between devices: 14.6 us -> 22.6 us
    psum x1 -> x0, waiting for transfers between devices: 356 us -> none  [shards(): source = lax.psum(partial_value.astype(jnp.bfloat16), 'chan')]
    all_to_all x2, waiting for transfers between devices: 134 us -> 36.8 us  [the longest x1 25.2 us: shards(): lax.all_to_all(encode(samples, source_index), 'chan', 0, 0, tiled=True)]
    unnamed x9 -> x26, local copies, waits for them, and re-layouts: 79.9 us -> 4.68 us
    pallas_call x0 -> x7, Pallas kernels: none -> 46.2 us  [the longest x2 17.6 us: transform(): pl.pallas_call(transform_kernel, grid_spec=pltpu.PrefetchScalarGridSpec(n...]
    dot_general x3 -> x0, matrix products: 42.3 us -> none  [the longest x1 24.3 us: transform(): jnp.einsum('kwc,wg->kgc', blocks, dft_rows, precision=lax.Precision.HIGHE...]
    all_to_all x3 -> x0, local copies, waits for them, and re-layouts: 22.5 us -> none  [the longest x2 20 us: shards(): lax.all_to_all(samples, 'chan', split_axis=2, concat_axis=1, tiled=True)]
    all_to_all x1 -> x0, other arithmetic: 19.4 us -> none  [shards(): lax.all_to_all(samples, 'chan', split_axis=2, concat_axis=1, tiled=True)]
  transfers between devices with their start and end apart: 3 -> 11, of which waited for: 3 -> 3; matrix products, arithmetic and copies ran while one was open for 1% -> 16% of each run, Pallas kernels for 0% -> 20%
where the time goes in v2:
time: 135 us; the launch traced here: 133 us
  Pallas kernels  46.2 us (34%)
  waiting for transfers between devices  37.8 us (28%)
  starting transfers between devices  22.6 us (17%)
  other arithmetic  19.3 us (14%)
  local copies, waits for them, and re-layouts  6.66 us (5%)
    all_to_all x1, waiting for transfers between devices, shards(): lax.all_to_all(encode(samples, source_index), 'chan', 0, 0, tiled=True)  25.2 us
    pallas_call x2, Pallas kernels, transform(): pl.pallas_call(transform_kernel, grid_spec=pltpu.PrefetchScalarGridSpec(n...  17.6 us
    mul x1, other arithmetic, dft_table(): table = taper * jnp.cos(phase.astype(f32) * (2.0 * math.pi / WIN))  15.8 us
    pallas_call x2, Pallas kernels, stack(): pl.pallas_call(functools.partial(stack_kernel, band), grid=(1,), in_specs...  13.6 us
    all_to_all x1, waiting for transfers between devices, shards(): lax.all_to_all(packed, 'chan', 0, 0, tiled=True, axis_index_groups=groups)  11.7 us
    all_to_all x1, starting transfers between devices, shards(): lax.all_to_all(encode(samples, source_index), 'chan', 0, 0, tiled=True)  10.7 us
    pallas_call x1, Pallas kernels, encode(): pl.pallas_call(encode_kernel, grid=(steps,), in_specs=[pl.BlockSpec((KW,...  7.07 us
    ppermute x9, starting transfers between devices, swap(): return lax.ppermute(value, axis, [(i, i ^ distance) for i in range(size)])  5.94 us
  transfers between devices with their start and end apart: 11, of which 3 were waited for; matrix products, arithmetic and copies ran while one was open for 16% of the time, Pallas kernels for 20%

profile of v2, /device:TPU:0, one launch (start us, length us, event | category | flops | bytes accessed | tf_op | source)
XLA Modules:
  0.0 133.0 jit_solution(9476964700727809173)
XLA Ops:
  0.0 7.1 %encode.1 = s16[32,208,256]{2,1,0:T(8,128)(2,1)} custom-call(f32[6,32,8192]{2,1,0:T(8,128)} %samples.1, s32[1,128]{1,0:T(1,128)} %bitcast.7), custom_call_target="tpu_custom_call" | custom-call | tf_op jit(solution)/shard_map/encode/pallas_call | solution.py:124
  7.1 0.0 copy-start.12
  7.1 0.0 copy-start.8
  7.1 10.7 %all-to-all-start = ((s16[32,208,256]{2,1,0:T(8,128)(2,1)}), s16[32,208,256]{2,1,0:T(8,128)(2,1)S(1)}, u32[]{:S(2)}, u32[]{:S(2)}) async-start(s16[32,208,256]{2,1,0:T(8,128)(2,1)} %encode.1), calls=%async_computation | async-start | bytes 6815744 | tf_op jit(solution)/shard_map/all_to_all | solution.py:381
  17.9 0.0 copy-done.12
  17.9 0.1 compare_select_fusion
  18.0 0.0 copy-done.8
  18.0 0.6 gather_fusion
  18.6 0.7 dynamic_slice.7
  19.3 0.7 reshape_tile.4.live
  20.0 15.8 %fusion.5 = f32[1024,1024]{1,0:T(8,128)S(1)} fusion(s32[1024]{0:T(1024)S(1)} %get-tuple-element.50, s32[1024]{0:T(1024)S(1)} %get-tuple-element.49, f32[1024]{0:T(1024)S(1)} %multiply_subtract_fusion), kind=kLoop, calls=%fused_computation.11 | loop fusion | flops 16777216 | bytes 4206592 | tf_op jit(solution)/shard_map/mul | solution.py:51
  35.8 0.9 reduce-precision_convert_fusion
  36.8 2.5 %pad_maximum_fusion.table = bf16[2,1024,1024]{2,1,0:T(8,128)(2,1)} fusion(bf16[2,512,1024]{2,1,0:T(8,128)(2,1)S(1)} %get-tuple-element.48, bf16[2,512,1024]{2,1,0:T(8,128)(2,1)S(1)} %get-tuple-element.47), kind=kLoop, calls=%fused_computation.12 | loop fusion | flops 8388608 | bytes 8388608 | tf_op jit(solution)/shard_map/concatenate | solution.py:54
  39.2 25.2 %all-to-all-done.extra.codes = s16[32,208,256]{2,1,0:T(8,128)(2,1)S(1)} async-done(((s16[32,208,256]{2,1,0:T(8,128)(2,1)}), s16[32,208,256]{2,1,0:T(8,128)(2,1)S(1)}, u32[]{:S(2)}, u32[]{:S(2)}) %all-to-all-start) | async-done | bytes 3407904 | tf_op jit(solution)/shard_map/all_to_all | solution.py:381
  64.4 1.7 %copy-done.1 = s16[32,208,256]{2,1,0:T(8,128)(2,1)} copy-done((s16[32,208,256]{2,1,0:T(8,128)(2,1)}, s16[32,208,256]{2,1,0:T(8,128)(2,1)S(1)}, u32[]{:S(2)}) %copy-start.1) | copy-done | bytes 3407896
  66.1 5.5 %sources.1 = (bf16[48,256]{1,0:T(8,128)(2,1)}, bf16[48,256]{1,0:T(8,128)(2,1)}, bf16[48,256]{1,0:T(8,128)(2,1)}, bf16[48,256]{1,0:T(8,128)(2,1)}) custom-call(s32[1]{0:T(128)} %bitcast.mine, s16[32,208,256]{2,1,0:T(8,128)(2,1)} %copy-done.1, bf16[2,1024,1024]{2,1,0:T(8,128)(2,1)} %pad_maximum_fusion.table, f32[48,1]{1,0:T(8,128)} %reshape_tile.4.live), custom_call_target="tpu_custom_call" | custom-call | tf_op jit(solution)/shard_map/sources/pallas_call | solution.py:229
  71.6 0.0 collective-permute-start
  71.6 1.0 collective-permute-start.1
  72.6 0.8 collective-permute-start.2
  73.4 8.8 %transform.2 = (bf16[768,256]{1,0:T(8,128)(2,1)}, bf16[768,256]{1,0:T(8,128)(2,1)}, bf16[768,256]{1,0:T(8,128)(2,1)}, bf16[768,256]{1,0:T(8,128)(2,1)}) custom-call(s32[1]{0:T(128)} %bitcast.mine, s16[32,208,256]{2,1,0:T(8,128)(2,1)} %copy-done.1, s16[32,208,256]{2,1,0:T(8,128)(2,1)} %copy-done.1, bf16[2,1024,1024]{2,1,0:T(8,128)(2,1)} %pad_maximum_fusion.table, ...), custom_call_target="tpu_custom_call" | custom-call | flops 40000000000 | bytes 100000000 | tf_op jit(solution)/shard_map/transform/pallas_call | solution.py:175
  82.2 0.0 collective-permute-done.b
  82.2 0.0 collective-permute-done.1.c
  82.2 0.0 copy-start.10
  82.3 0.0 collective-permute-done.2.d
  82.3 0.4 collective-permute-start.8
  82.6 0.9 collective-permute-start.4
  83.5 1.0 collective-permute-start.3
  84.5 2.5 %pack.1 = bf16[16,2,192,128]{3,2,1,0:T(8,128)(2,1)} custom-call(bf16[48,256]{1,0:T(8,128)(2,1)} %get-tuple-element.29.a, bf16[48,256]{1,0:T(8,128)(2,1)} %copy-done.9, bf16[48,256]{1,0:T(8,128)(2,1)} %copy-done.10, bf16[48,256]{1,0:T(8,128)(2,1)} %copy-done.11), custom_call_target="tpu_custom_call" | custom-call | tf_op jit(solution)/shard_map/pack/pallas_call | solution.py:271
  87.0 5.9 %all-to-all-start.1 = ((bf16[16,2,192,128]{3,2,1,0:T(8,128)(2,1)}), bf16[16,2,192,128]{3,2,1,0:T(8,128)(2,1)S(1)}, u32[]{:S(2)}, u32[]{:S(2)}) async-start(bf16[16,2,192,128]{3,2,1,0:T(8,128)(2,1)} %pack.1), calls=%async_computation.1 | async-start | bytes 3145728 | tf_op jit(solution)/shard_map/all_to_all | solution.py:388
  92.9 8.8 %transform.3 = (bf16[768,256]{1,0:T(8,128)(2,1)}, bf16[768,256]{1,0:T(8,128)(2,1)}, bf16[768,256]{1,0:T(8,128)(2,1)}, bf16[768,256]{1,0:T(8,128)(2,1)}) custom-call(s32[1]{0:T(128)} %bitcast.mine, s16[32,208,256]{2,1,0:T(8,128)(2,1)} %copy-done.1, s16[32,208,256]{2,1,0:T(8,128)(2,1)} %copy-done.1, bf16[2,1024,1024]{2,1,0:T(8,128)(2,1)} %pad_maximum_fusion.table, ...), custom_call_target="tpu_custom_call" | custom-call | flops 40000000000 | bytes 100000000 | tf_op jit(solution)/shard_map/transform/pallas_call | solution.py:175
  101.7 0.0 collective-permute-done.4.d
  101.7 0.9 collective-permute-done.3.c
  102.7 0.8 copy-done.7
  103.4 0.4 collective-permute-start.7
  103.9 1.0 collective-permute-start.6
  104.9 0.4 collective-permute-start.5
  105.3 0.0 collective-permute-done.8.b
  105.3 11.7 %all-to-all-done.1.sources = bf16[16,2,192,128]{3,2,1,0:T(8,128)(2,1)S(1)} async-done(((bf16[16,2,192,128]{3,2,1,0:T(8,128)(2,1)}), bf16[16,2,192,128]{3,2,1,0:T(8,128)(2,1)S(1)}, u32[]{:S(2)}, u32[]{:S(2)}) %all-to-all-start.1) | async-done | bytes 1572896 | tf_op jit(solution)/shard_map/all_to_all | solution.py:388
  117.0 1.2 copy-done
  118.2 6.8 %stack.2.rest_0_ = bf16[128,2,128,256]{3,2,1,0:T(8,128)(2,1)} custom-call(bf16[16,2,192,128]{3,2,1,0:T(8,128)(2,1)} %copy-done, bf16[768,256]{1,0:T(8,128)(2,1)} %get-tuple-element.28.a, bf16[768,256]{1,0:T(8,128)(2,1)} %copy-done.5, bf16[768,256]{1,0:T(8,128)(2,1)} %copy-done.7, bf16[768,256]{1,0:T(8,128)(2,1)} %copy-done.6), custom_call_target="tpu_custom_call" | custom-call | tf_op jit(solution)/shard_map/stack/pallas_call | solution.py:344
  125.0 0.0 collective-permute-done.7.d
  125.0 0.0 copy-start.2
  125.0 0.0 collective-permute-done.6.c
  125.0 0.0 collective-permute-done.5.b
  125.0 0.7 copy-done.2
  125.7 0.1 copy-done.3
  125.9 0.1 copy-done.4
  126.0 6.8 %stack.3 = bf16[128,2,128,256]{3,2,1,0:T(8,128)(2,1)} custom-call(bf16[16,2,192,128]{3,2,1,0:T(8,128)(2,1)} %copy-done, bf16[768,256]{1,0:T(8,128)(2,1)} %get-tuple-element.34.a, bf16[768,256]{1,0:T(8,128)(2,1)} %copy-done.4, bf16[768,256]{1,0:T(8,128)(2,1)} %copy-done.3, bf16[768,256]{1,0:T(8,128)(2,1)} %copy-done.2, ...), custom_call_target="tpu_custom_call", output_to_operand_aliasing={{}: (5, {})} | custom-call | tf_op jit(solution)/shard_map/stack/pallas_call | solution.py:344
  (19 shorter events, 0.1 us)
Async XLA Ops:
  7.1 10.8 %copy-start.12 = (s32[128]{0:T(128)S(1)}, s32[128]{0:T(128)}, u32[]{:S(2)}) copy-start(s32[128]{0:T(128)} %param.4) | copy-start | bytes 1540
  7.1 10.9 %copy-start.8 = (s32[8192]{0:T(1024)S(1)}, s32[8192]{0:T(1024)}, u32[]{:S(2)}) copy-start(s32[8192]{0:T(1024)} %param.5) | copy-start | bytes 98308
  7.1 57.3 %all-to-all-start = ((s16[32,208,256]{2,1,0:T(8,128)(2,1)}), s16[32,208,256]{2,1,0:T(8,128)(2,1)S(1)}, u32[]{:S(2)}, u32[]{:S(2)}) async-start(s16[32,208,256]{2,1,0:T(8,128)(2,1)} %encode.1), calls=%async_computation | async-start | bytes 6815744 | tf_op jit(solution)/shard_map/all_to_all | solution.py:381
  64.4 1.7 %copy-start.1 = (s16[32,208,256]{2,1,0:T(8,128)(2,1)}, s16[32,208,256]{2,1,0:T(8,128)(2,1)S(1)}, u32[]{:S(2)}) copy-start(s16[32,208,256]{2,1,0:T(8,128)(2,1)S(1)} %all-to-all-done.extra.codes) | copy-start | bytes 10223620
  71.6 10.7 %collective-permute-start = (bf16[48,256]{1,0:T(8,128)(2,1)}, bf16[48,256]{1,0:T(8,128)(2,1)S(1)}, u32[]{:S(2)}, u32[]{:S(2)}) collective-permute-start(bf16[48,256]{1,0:T(8,128)(2,1)} %get-tuple-element.30), channel_id=1, source_target_pairs={{0,32},{32,0},{64,96},{96,64},{1,33},{33,1},{65,97},{97,65},{2,34}... | collective-permute-start | bytes 73736 | tf_op jit(solution)/shard_map/ppermute | solution.py:364
  71.6 10.7 %collective-permute-start.1 = (bf16[48,256]{1,0:T(8,128)(2,1)}, bf16[48,256]{1,0:T(8,128)(2,1)S(1)}, u32[]{:S(2)}, u32[]{:S(2)}) collective-permute-start(bf16[48,256]{1,0:T(8,128)(2,1)} %get-tuple-element.31), channel_id=1, source_target_pairs={{0,64},{32,96},{64,0},{96,32},{1,65},{33,97},{65,1},{97,33},{2,66}... | collective-permute-start | bytes 73736 | tf_op jit(solution)/shard_map/ppermute | solution.py:364
  72.6 9.7 %collective-permute-start.2 = (bf16[48,256]{1,0:T(8,128)(2,1)}, bf16[48,256]{1,0:T(8,128)(2,1)S(1)}, u32[]{:S(2)}, u32[]{:S(2)}) collective-permute-start(bf16[48,256]{1,0:T(8,128)(2,1)} %get-tuple-element.32), channel_id=1, source_target_pairs={{0,96},{32,64},{64,32},{96,0},{1,97},{33,65},{65,33},{97,1},{2,98}... | collective-permute-start | bytes 73736 | tf_op jit(solution)/shard_map/ppermute | solution.py:364
  82.2 2.3 %copy-start.9 = (bf16[48,256]{1,0:T(8,128)(2,1)}, bf16[48,256]{1,0:T(8,128)(2,1)S(1)}, u32[]{:S(2)}) copy-start(bf16[48,256]{1,0:T(8,128)(2,1)S(1)} %collective-permute-done.b) | copy-start | bytes 73732
  82.2 2.3 %copy-start.10 = (bf16[48,256]{1,0:T(8,128)(2,1)}, bf16[48,256]{1,0:T(8,128)(2,1)S(1)}, u32[]{:S(2)}) copy-start(bf16[48,256]{1,0:T(8,128)(2,1)S(1)} %collective-permute-done.1.c) | copy-start | bytes 73732
  82.3 2.2 %copy-start.11 = (bf16[48,256]{1,0:T(8,128)(2,1)}, bf16[48,256]{1,0:T(8,128)(2,1)S(1)}, u32[]{:S(2)}) copy-start(bf16[48,256]{1,0:T(8,128)(2,1)S(1)} %collective-permute-done.2.d) | copy-start | bytes 73732
  82.3 23.0 %collective-permute-start.8 = (bf16[768,256]{1,0:T(8,128)(2,1)}, bf16[768,256]{1,0:T(8,128)(2,1)S(1)}, u32[]{:S(2)}, u32[]{:S(2)}) collective-permute-start(bf16[768,256]{1,0:T(8,128)(2,1)} %get-tuple-element.46), channel_id=1, source_target_pairs={{0,32},{32,0},{64,96},{96,64},{1,33},{33,1},{65,97},{97,65},{2,34}... | collective-permute-start | bytes 1179656 | tf_op jit(solution)/shard_map/ppermute | solution.py:364
  82.6 19.1 %collective-permute-start.4 = (bf16[768,256]{1,0:T(8,128)(2,1)}, bf16[768,256]{1,0:T(8,128)(2,1)S(1)}, u32[]{:S(2)}, u32[]{:S(2)}) collective-permute-start(bf16[768,256]{1,0:T(8,128)(2,1)} %get-tuple-element.39), channel_id=1, source_target_pairs={{0,96},{32,64},{64,32},{96,0},{1,97},{33,65},{65,33},{97,1},{2,98}... | collective-permute-start | bytes 1179656 | tf_op jit(solution)/shard_map/ppermute | solution.py:364
  83.5 19.2 %collective-permute-start.3 = (bf16[768,256]{1,0:T(8,128)(2,1)}, bf16[768,256]{1,0:T(8,128)(2,1)S(1)}, u32[]{:S(2)}, u32[]{:S(2)}) collective-permute-start(bf16[768,256]{1,0:T(8,128)(2,1)} %get-tuple-element.37), channel_id=1, source_target_pairs={{0,64},{32,96},{64,0},{96,32},{1,65},{33,97},{65,1},{97,33},{2,66}... | collective-permute-start | bytes 1179656 | tf_op jit(solution)/shard_map/ppermute | solution.py:364
  87.0 30.0 %all-to-all-start.1 = ((bf16[16,2,192,128]{3,2,1,0:T(8,128)(2,1)}), bf16[16,2,192,128]{3,2,1,0:T(8,128)(2,1)S(1)}, u32[]{:S(2)}, u32[]{:S(2)}) async-start(bf16[16,2,192,128]{3,2,1,0:T(8,128)(2,1)} %pack.1), calls=%async_computation.1 | async-start | bytes 3145728 | tf_op jit(solution)/shard_map/all_to_all | solution.py:388
  101.7 15.2 %copy-start.6 = (bf16[768,256]{1,0:T(8,128)(2,1)}, bf16[768,256]{1,0:T(8,128)(2,1)S(1)}, u32[]{:S(2)}) copy-start(bf16[768,256]{1,0:T(8,128)(2,1)S(1)} %collective-permute-done.4.d) | copy-start | bytes 1179652
  102.7 0.8 copy-start.7
  103.4 21.5 %collective-permute-start.7 = (bf16[768,256]{1,0:T(8,128)(2,1)}, bf16[768,256]{1,0:T(8,128)(2,1)S(1)}, u32[]{:S(2)}, u32[]{:S(2)}) collective-permute-start(bf16[768,256]{1,0:T(8,128)(2,1)} %get-tuple-element.44), channel_id=1, source_target_pairs={{0,96},{32,64},{64,32},{96,0},{1,97},{33,65},{65,33},{97,1},{2,98}... | collective-permute-start | bytes 1179656 | tf_op jit(solution)/shard_map/ppermute | solution.py:364
  103.9 21.1 %collective-permute-start.6 = (bf16[768,256]{1,0:T(8,128)(2,1)}, bf16[768,256]{1,0:T(8,128)(2,1)S(1)}, u32[]{:S(2)}, u32[]{:S(2)}) collective-permute-start(bf16[768,256]{1,0:T(8,128)(2,1)} %get-tuple-element.42), channel_id=1, source_target_pairs={{0,64},{32,96},{64,0},{96,32},{1,65},{33,97},{65,1},{97,33},{2,66}... | collective-permute-start | bytes 1179656 | tf_op jit(solution)/shard_map/ppermute | solution.py:364
  104.9 20.1 %collective-permute-start.5 = (bf16[768,256]{1,0:T(8,128)(2,1)}, bf16[768,256]{1,0:T(8,128)(2,1)S(1)}, u32[]{:S(2)}, u32[]{:S(2)}) collective-permute-start(bf16[768,256]{1,0:T(8,128)(2,1)} %get-tuple-element.40), channel_id=1, source_target_pairs={{0,32},{32,0},{64,96},{96,64},{1,33},{33,1},{65,97},{97,65},{2,34}... | collective-permute-start | bytes 1179656 | tf_op jit(solution)/shard_map/ppermute | solution.py:364
  105.3 11.7 %copy-start.5 = (bf16[768,256]{1,0:T(8,128)(2,1)}, bf16[768,256]{1,0:T(8,128)(2,1)S(1)}, u32[]{:S(2)}) copy-start(bf16[768,256]{1,0:T(8,128)(2,1)S(1)} %collective-permute-done.8.b) | copy-start | bytes 1179652
  117.0 1.2 copy-start
  125.0 0.8 copy-start.2
  125.0 0.9 copy-start.3
  125.0 1.0 copy-start.4

commit v3 on v2

--- a/solution.py
+++ b/solution.py
@@ -29,6 +29,9 @@
 ROUND = 1.5 * 2.0**23
 EPS = 1e-06
 VMEM = 56 * 1024 * 1024
+VMEM_LESS = 46 * 1024 * 1024
+VMEM_LEAST = 40 * 1024 * 1024
+LONG = pl.CostEstimate(flops=40 * 10**9, bytes_accessed=10**8, transcendentals=0)
 
 f32 = jnp.float32
 bf16 = jnp.bfloat16
@@ -188,7 +191,7 @@
         ),
         out_shape=shapes,
         compiler_params=pltpu.CompilerParams(vmem_limit_bytes=VMEM),
-        cost_estimate=pl.CostEstimate(flops=40 * 10**9, bytes_accessed=10**8, transcendentals=0),
+        cost_estimate=LONG,
         name="transform",
     )(mine, received, received, table, live)
 
@@ -238,7 +241,7 @@
         out_specs=[piece] * TM,
         out_shape=[jax.ShapeDtypeStruct((KW * PICK, WIDTH), bf16)] * TM,
         scratch_shapes=[pltpu.VMEM((KW * PICK, WIN), f32), pltpu.VMEM((2, TM, KW * PICK, rows), f32)],
-        compiler_params=pltpu.CompilerParams(vmem_limit_bytes=VMEM),
+        compiler_params=pltpu.CompilerParams(vmem_limit_bytes=VMEM_LEAST),
         name="sources",
     )(mine, received, table, live)
 
@@ -273,7 +276,7 @@
         in_specs=[whole] * TM,
         out_specs=whole,
         out_shape=jax.ShapeDtypeStruct((NEAR, 2, 24 * PICK, 128), bf16),
-        compiler_params=pltpu.CompilerParams(vmem_limit_bytes=VMEM),
+        compiler_params=pltpu.CompilerParams(vmem_limit_bytes=VMEM_LESS),
         name="pack",
     )(*spectra)
 
@@ -329,7 +332,7 @@
         copy(g).start()
         return carry
 
-    lax.fori_loop(0, steps, body, 0)
+    lax.fori_loop(0, steps, body, 0, unroll=True)
 
     def finish(g, carry):
         copy(g).wait()
@@ -355,7 +358,7 @@
             pltpu.SemaphoreType.DMA((BAND // GROUP // 2,)),
         ],
         input_output_aliases={} if before is None else {1 + TM: 0},
-        compiler_params=pltpu.CompilerParams(vmem_limit_bytes=VMEM),
+        compiler_params=pltpu.CompilerParams(vmem_limit_bytes=VMEM_LESS),
         name="stack",
     )(sources, *parts, *extra)
 
@@ -388,7 +391,7 @@
     left = lax.all_to_all(packed, "chan", 0, 0, tiled=True, axis_index_groups=groups)
     pieces = transform(mine, after(received, packed), table, live, 1)
     second = [pieces[0]] + [
-        swap(after(pieces[k], *first[2:]), "tm", TM, k) for k in range(1, TM)
+        swap(pieces[k], "tm", TM, k) for k in range(1, TM)
     ]
     result = stack(left, first, 0, None)
     return stack(left, second, 1, result)

time: 135 us -> 127 us (0.941)
  Pallas kernels: 46.2 us -> 37.9 us
  waiting for transfers between devices: 37.8 us -> 39.6 us
    pallas_call x2, Pallas kernels: 13.6 us -> 8.86 us  [stack(): pl.pallas_call(functools.partial(stack_kernel, band), grid=(1,), in_specs...]
    pallas_call x1, Pallas kernels: 5.48 us -> 2.55 us  [sources(): pl.pallas_call(sources_kernel, grid=(1,), in_specs=[pl.BlockSpec(memory_s...]
    all_to_all x1, waiting for transfers between devices: 11.7 us -> 13.8 us  [shards(): lax.all_to_all(packed, 'chan', 0, 0, tiled=True, axis_index_groups=groups)]
    unnamed x26 -> x16, local copies, waits for them, and re-layouts: 4.68 us -> 5.18 us
  transfers between devices with their start and end apart: 11 -> 11, of which waited for: 3 -> 2; matrix products, arithmetic and copies ran while one was open for 16% -> 16% of each run, Pallas kernels for 20% -> 19%
where the time goes in v3:
time: 127 us; the launch traced here: 126 us
  waiting for transfers between devices  39.6 us (31%)
  Pallas kernels  37.9 us (30%)
  starting transfers between devices  22.6 us (18%)
  other arithmetic  19.3 us (15%)
  local copies, waits for them, and re-layouts  6.52 us (5%)
    all_to_all x1, waiting for transfers between devices, shards(): lax.all_to_all(encode(samples, source_index), 'chan', 0, 0, tiled=True)  25.8 us
    pallas_call x2, Pallas kernels, transform(): pl.pallas_call(transform_kernel, grid_spec=pltpu.PrefetchScalarGridSpec(n...  17.7 us
    mul x1, other arithmetic, dft_table(): table = taper * jnp.cos(phase.astype(f32) * (2.0 * math.pi / WIN))  15.8 us
    all_to_all x1, waiting for transfers between devices, shards(): lax.all_to_all(packed, 'chan', 0, 0, tiled=True, axis_index_groups=groups)  13.8 us
    all_to_all x1, starting transfers between devices, shards(): lax.all_to_all(encode(samples, source_index), 'chan', 0, 0, tiled=True)  10.7 us
    pallas_call x2, Pallas kernels, stack(): pl.pallas_call(functools.partial(stack_kernel, band), grid=(1,), in_specs...  8.86 us
    pallas_call x1, Pallas kernels, encode(): pl.pallas_call(encode_kernel, grid=(steps,), in_specs=[pl.BlockSpec((KW,...  7.11 us
    all_to_all x1, starting transfers between devices, shards(): lax.all_to_all(packed, 'chan', 0, 0, tiled=True, axis_index_groups=groups)  5.94 us
  transfers between devices with their start and end apart: 11, of which 2 were waited for; matrix products, arithmetic and copies ran while one was open for 16% of the time, Pallas kernels for 19%

profile of v3, /device:TPU:0, one launch (start us, length us, event | category | flops | bytes accessed | tf_op | source)
XLA Modules:
  0.0 126.3 jit_solution(11897992760029678939)
XLA Ops:
  0.0 7.1 %encode.1 = s16[32,208,256]{2,1,0:T(8,128)(2,1)} custom-call(f32[6,32,8192]{2,1,0:T(8,128)} %samples.1, s32[1,128]{1,0:T(1,128)} %bitcast.7), custom_call_target="tpu_custom_call" | custom-call | tf_op jit(solution)/shard_map/encode/pallas_call | solution.py:127
  7.1 0.0 copy-start.7
  7.1 0.0 copy-start.6
  7.1 10.7 %all-to-all-start = ((s16[32,208,256]{2,1,0:T(8,128)(2,1)}), s16[32,208,256]{2,1,0:T(8,128)(2,1)S(1)}, u32[]{:S(2)}, u32[]{:S(2)}) async-start(s16[32,208,256]{2,1,0:T(8,128)(2,1)} %encode.1), calls=%async_computation | async-start | bytes 6815744 | tf_op jit(solution)/shard_map/all_to_all | solution.py:384
  17.9 0.0 copy-done.7
  17.9 0.1 compare_select_fusion
  18.0 0.0 copy-done.6
  18.0 0.6 gather_fusion
  18.7 0.6 dynamic_slice.7
  19.3 0.1 reshape_tile.4.live
  19.4 15.8 %fusion.5 = f32[1024,1024]{1,0:T(8,128)S(1)} fusion(s32[1024]{0:T(1024)S(1)} %get-tuple-element.44, s32[1024]{0:T(1024)S(1)} %get-tuple-element.43, f32[1024]{0:T(1024)S(1)} %multiply_subtract_fusion), kind=kLoop, calls=%fused_computation.11 | loop fusion | flops 16777216 | bytes 4206592 | tf_op jit(solution)/shard_map/mul | solution.py:54
  35.2 0.9 reduce-precision_convert_fusion
  36.2 2.5 %pad_maximum_fusion.table = bf16[2,1024,1024]{2,1,0:T(8,128)(2,1)} fusion(bf16[2,512,1024]{2,1,0:T(8,128)(2,1)S(1)} %get-tuple-element.42, bf16[2,512,1024]{2,1,0:T(8,128)(2,1)S(1)} %get-tuple-element.41), kind=kLoop, calls=%fused_computation.12 | loop fusion | flops 8388608 | bytes 8388608 | tf_op jit(solution)/shard_map/concatenate | solution.py:57
  38.6 25.8 %all-to-all-done.extra.codes = s16[32,208,256]{2,1,0:T(8,128)(2,1)S(1)} async-done(((s16[32,208,256]{2,1,0:T(8,128)(2,1)}), s16[32,208,256]{2,1,0:T(8,128)(2,1)S(1)}, u32[]{:S(2)}, u32[]{:S(2)}) %all-to-all-start) | async-done | bytes 3407904 | tf_op jit(solution)/shard_map/all_to_all | solution.py:384
  64.4 0.0 copy-start.1
  64.4 3.4 %copy-done = bf16[2,1024,1024]{2,1,0:T(8,128)(2,1)S(1)} copy-done((bf16[2,1024,1024]{2,1,0:T(8,128)(2,1)S(1)}, bf16[2,1024,1024]{2,1,0:T(8,128)(2,1)}, u32[]{:S(2)}) %copy-start) | copy-done | bytes 4194328
  67.8 2.5 %sources.1 = (bf16[48,256]{1,0:T(8,128)(2,1)S(1)}, bf16[48,256]{1,0:T(8,128)(2,1)S(1)}, bf16[48,256]{1,0:T(8,128)(2,1)S(1)}, bf16[48,256]{1,0:T(8,128)(2,1)S(1)}) custom-call(s32[1]{0:T(128)} %bitcast.mine, s16[32,208,256]{2,1,0:T(8,128)(2,1)S(1)} %all-to-all-done.extra.codes, bf16[2,1024,1024]{2,1,0:T(8,128)(2,1)S(1)} %copy-done, f32[48,1]{1,0:T(8,128)S(1)} %reshape_tile.4.live), custom_call_target="tpu_custom_call" | custom-call | tf_op jit(solution)/shard_map/sources/pallas_call | solution.py:232
  70.4 0.1 collective-permute-start
  70.5 1.1 collective-permute-start.1
  71.6 0.8 collective-permute-start.2
  72.3 0.0 copy-done.1
  72.3 8.9 %transform.2 = (bf16[768,256]{1,0:T(8,128)(2,1)}, bf16[768,256]{1,0:T(8,128)(2,1)}, bf16[768,256]{1,0:T(8,128)(2,1)}, bf16[768,256]{1,0:T(8,128)(2,1)}) custom-call(s32[1]{0:T(128)} %bitcast.mine, s16[32,208,256]{2,1,0:T(8,128)(2,1)} %copy-done.1, s16[32,208,256]{2,1,0:T(8,128)(2,1)} %copy-done.1, bf16[2,1024,1024]{2,1,0:T(8,128)(2,1)} %pad_maximum_fusion.table, ...), custom_call_target="tpu_custom_call" | custom-call | flops 40000000000 | bytes 100000000 | tf_op jit(solution)/shard_map/transform/pallas_call | solution.py:178
  81.2 0.0 collective-permute-done.b
  81.2 0.0 collective-permute-done.1.c
  81.2 0.0 collective-permute-done.2.d
  81.2 1.1 collective-permute-start.8
  82.3 1.0 collective-permute-start.7
  83.3 0.0 collective-permute-start.6
  83.3 1.6 %pack.1 = bf16[16,2,192,128]{3,2,1,0:T(8,128)(2,1)} custom-call(bf16[48,256]{1,0:T(8,128)(2,1)S(1)} %get-tuple-element.26.a, bf16[48,256]{1,0:T(8,128)(2,1)S(1)} %collective-permute-done.b, bf16[48,256]{1,0:T(8,128)(2,1)S(1)} %collective-permute-done.1.c, bf16[48,256]{1,0:T(8,128)(2,1)S(1)} %collective-permute-done.2.d), custom_call_target="tpu_custom_call" | custom-call | tf_op jit(solution)/shard_map/pack/pallas_call | solution.py:274
  84.9 5.9 %all-to-all-start.1 = ((bf16[16,2,192,128]{3,2,1,0:T(8,128)(2,1)}), bf16[16,2,192,128]{3,2,1,0:T(8,128)(2,1)S(1)}, u32[]{:S(2)}, u32[]{:S(2)}) async-start(bf16[16,2,192,128]{3,2,1,0:T(8,128)(2,1)} %pack.1), calls=%async_computation.1 | async-start | bytes 3145728 | tf_op jit(solution)/shard_map/all_to_all | solution.py:391
  90.9 0.0 copy-start.3
  90.9 8.9 %transform.3 = (bf16[768,256]{1,0:T(8,128)(2,1)}, bf16[768,256]{1,0:T(8,128)(2,1)}, bf16[768,256]{1,0:T(8,128)(2,1)}, bf16[768,256]{1,0:T(8,128)(2,1)}) custom-call(s32[1]{0:T(128)} %bitcast.mine, s16[32,208,256]{2,1,0:T(8,128)(2,1)} %copy-done.1, s16[32,208,256]{2,1,0:T(8,128)(2,1)} %copy-done.1, bf16[2,1024,1024]{2,1,0:T(8,128)(2,1)} %pad_maximum_fusion.table, ...), custom_call_target="tpu_custom_call" | custom-call | flops 40000000000 | bytes 100000000 | tf_op jit(solution)/shard_map/transform/pallas_call | solution.py:178
  99.8 0.2 collective-permute-start.3
  100.0 1.0 collective-permute-start.4
  101.0 0.0 collective-permute-done.8.d
  101.0 0.7 copy-done.4
  101.8 0.6 collective-permute-start.5
  102.4 0.0 collective-permute-done.7.c
  102.4 0.0 collective-permute-done.6.b
  102.4 13.8 %all-to-all-done.1.sources = bf16[16,2,192,128]{3,2,1,0:T(8,128)(2,1)S(1)} async-done(((bf16[16,2,192,128]{3,2,1,0:T(8,128)(2,1)}), bf16[16,2,192,128]{3,2,1,0:T(8,128)(2,1)S(1)}, u32[]{:S(2)}, u32[]{:S(2)}) %all-to-all-start.1) | async-done | bytes 1572896 | tf_op jit(solution)/shard_map/all_to_all | solution.py:391
  116.2 0.0 copy-done.3
  116.2 1.0 copy-done.5
  117.2 5.0 %stack.2.rest_0_ = bf16[128,2,128,256]{3,2,1,0:T(8,128)(2,1)} custom-call(bf16[16,2,192,128]{3,2,1,0:T(8,128)(2,1)S(1)} %all-to-all-done.1.sources, bf16[768,256]{1,0:T(8,128)(2,1)S(1)} %copy-done.3, bf16[768,256]{1,0:T(8,128)(2,1)} %collective-permute-done.6.b, bf16[768,256]{1,0:T(8,128)(2,1)} %collective-permute-done.7.c, bf16[768,256]{1,0:T(8,128)(2,1)S(1)} %copy-done.5), custom_call_target="tpu_custom_call" | custom-call | tf_op jit(solution)/shard_map/stack/pallas_call | solution.py:347
  122.2 0.0 collective-permute-done.3.b
  122.2 0.0 collective-permute-done.4.c
  122.2 0.0 collective-permute-done.5.d
  122.2 0.0 copy-done.2
  122.2 3.9 %stack.3 = bf16[128,2,128,256]{3,2,1,0:T(8,128)(2,1)} custom-call(bf16[16,2,192,128]{3,2,1,0:T(8,128)(2,1)S(1)} %all-to-all-done.1.sources, bf16[768,256]{1,0:T(8,128)(2,1)S(1)} %copy-done.2, bf16[768,256]{1,0:T(8,128)(2,1)S(1)} %collective-permute-done.3.b, bf16[768,256]{1,0:T(8,128)(2,1)S(1)} %collective-permute-done.4.c, ...), custom_call_target="tpu_custom_call", output_to_operand_aliasing={{}: (5, {})} | custom-call | tf_op jit(solution)/shard_map/stack/pallas_call | solution.py:347
  (9 shorter events, 0.1 us)
Async XLA Ops:
  7.1 10.8 %copy-start.7 = (s32[128]{0:T(128)S(1)}, s32[128]{0:T(128)}, u32[]{:S(2)}) copy-start(s32[128]{0:T(128)} %param.4) | copy-start | bytes 1540
  7.1 10.9 %copy-start.6 = (s32[8192]{0:T(1024)S(1)}, s32[8192]{0:T(1024)}, u32[]{:S(2)}) copy-start(s32[8192]{0:T(1024)} %param.5) | copy-start | bytes 98308
  7.1 57.3 %all-to-all-start = ((s16[32,208,256]{2,1,0:T(8,128)(2,1)}), s16[32,208,256]{2,1,0:T(8,128)(2,1)S(1)}, u32[]{:S(2)}, u32[]{:S(2)}) async-start(s16[32,208,256]{2,1,0:T(8,128)(2,1)} %encode.1), calls=%async_computation | async-start | bytes 6815744 | tf_op jit(solution)/shard_map/all_to_all | solution.py:384
  64.4 7.9 %copy-start.1 = (s16[32,208,256]{2,1,0:T(8,128)(2,1)}, s16[32,208,256]{2,1,0:T(8,128)(2,1)S(1)}, u32[]{:S(2)}) copy-start(s16[32,208,256]{2,1,0:T(8,128)(2,1)S(1)} %all-to-all-done.extra.codes) | copy-start | bytes 10223620
  64.4 3.4 %copy-start = (bf16[2,1024,1024]{2,1,0:T(8,128)(2,1)S(1)}, bf16[2,1024,1024]{2,1,0:T(8,128)(2,1)}, u32[]{:S(2)}) copy-start(bf16[2,1024,1024]{2,1,0:T(8,128)(2,1)} %pad_maximum_fusion.table) | copy-start | bytes 12582916
  70.4 10.8 %collective-permute-start = (bf16[48,256]{1,0:T(8,128)(2,1)S(1)}, bf16[48,256]{1,0:T(8,128)(2,1)S(1)}, u32[]{:S(2)}, u32[]{:S(2)}) collective-permute-start(bf16[48,256]{1,0:T(8,128)(2,1)S(1)} %get-tuple-element.27), channel_id=1, source_target_pairs={{0,32},{32,0},{64,96},{96,64},{1,33},{33,1},{65,97},{97,65},{2,34}... | collective-permute-start | bytes 73736 | tf_op jit(solution)/shard_map/ppermute | solution.py:367
  70.5 10.7 %collective-permute-start.1 = (bf16[48,256]{1,0:T(8,128)(2,1)S(1)}, bf16[48,256]{1,0:T(8,128)(2,1)S(1)}, u32[]{:S(2)}, u32[]{:S(2)}) collective-permute-start(bf16[48,256]{1,0:T(8,128)(2,1)S(1)} %get-tuple-element.28), channel_id=1, source_target_pairs={{0,64},{32,96},{64,0},{96,32},{1,65},{33,97},{65,1},{97,33},{2,66}... | collective-permute-start | bytes 73736 | tf_op jit(solution)/shard_map/ppermute | solution.py:367
  71.6 9.6 %collective-permute-start.2 = (bf16[48,256]{1,0:T(8,128)(2,1)S(1)}, bf16[48,256]{1,0:T(8,128)(2,1)S(1)}, u32[]{:S(2)}, u32[]{:S(2)}) collective-permute-start(bf16[48,256]{1,0:T(8,128)(2,1)S(1)} %get-tuple-element.29), channel_id=1, source_target_pairs={{0,96},{32,64},{64,32},{96,0},{1,97},{33,65},{65,33},{97,1},{2,98}... | collective-permute-start | bytes 73736 | tf_op jit(solution)/shard_map/ppermute | solution.py:367
  81.2 19.8 %collective-permute-start.8 = (bf16[768,256]{1,0:T(8,128)(2,1)}, bf16[768,256]{1,0:T(8,128)(2,1)S(1)}, u32[]{:S(2)}, u32[]{:S(2)}) collective-permute-start(bf16[768,256]{1,0:T(8,128)(2,1)} %get-tuple-element.40), channel_id=1, source_target_pairs={{0,96},{32,64},{64,32},{96,0},{1,97},{33,65},{65,33},{97,1},{2,98}... | collective-permute-start | bytes 1179656 | tf_op jit(solution)/shard_map/ppermute | solution.py:367
  82.3 20.1 %collective-permute-start.7 = (bf16[768,256]{1,0:T(8,128)(2,1)}, bf16[768,256]{1,0:T(8,128)(2,1)}, u32[]{:S(2)}, u32[]{:S(2)}) collective-permute-start(bf16[768,256]{1,0:T(8,128)(2,1)} %get-tuple-element.38), channel_id=1, source_target_pairs={{0,64},{32,96},{64,0},{96,32},{1,65},{33,97},{65,1},{97,33},{2,66}... | collective-permute-start | bytes 1179656 | tf_op jit(solution)/shard_map/ppermute | solution.py:367
  83.3 19.1 %collective-permute-start.6 = (bf16[768,256]{1,0:T(8,128)(2,1)}, bf16[768,256]{1,0:T(8,128)(2,1)}, u32[]{:S(2)}, u32[]{:S(2)}) collective-permute-start(bf16[768,256]{1,0:T(8,128)(2,1)} %get-tuple-element.36), channel_id=1, source_target_pairs={{0,32},{32,0},{64,96},{96,64},{1,33},{33,1},{65,97},{97,65},{2,34}... | collective-permute-start | bytes 1179656 | tf_op jit(solution)/shard_map/ppermute | solution.py:367
  84.9 31.3 %all-to-all-start.1 = ((bf16[16,2,192,128]{3,2,1,0:T(8,128)(2,1)}), bf16[16,2,192,128]{3,2,1,0:T(8,128)(2,1)S(1)}, u32[]{:S(2)}, u32[]{:S(2)}) async-start(bf16[16,2,192,128]{3,2,1,0:T(8,128)(2,1)} %pack.1), calls=%async_computation.1 | async-start | bytes 3145728 | tf_op jit(solution)/shard_map/all_to_all | solution.py:391
  90.9 25.3 %copy-start.3 = (bf16[768,256]{1,0:T(8,128)(2,1)S(1)}, bf16[768,256]{1,0:T(8,128)(2,1)}, u32[]{:S(2)}) copy-start(bf16[768,256]{1,0:T(8,128)(2,1)} %get-tuple-element.25.a) | copy-start | bytes 1179652
  99.8 22.4 %collective-permute-start.3 = (bf16[768,256]{1,0:T(8,128)(2,1)}, bf16[768,256]{1,0:T(8,128)(2,1)S(1)}, u32[]{:S(2)}, u32[]{:S(2)}) collective-permute-start(bf16[768,256]{1,0:T(8,128)(2,1)} %get-tuple-element.32), channel_id=1, source_target_pairs={{0,32},{32,0},{64,96},{96,64},{1,33},{33,1},{65,97},{97,65},{2,34}... | collective-permute-start | bytes 1179656 | tf_op jit(solution)/shard_map/ppermute | solution.py:367
  100.0 22.2 %collective-permute-start.4 = (bf16[768,256]{1,0:T(8,128)(2,1)}, bf16[768,256]{1,0:T(8,128)(2,1)S(1)}, u32[]{:S(2)}, u32[]{:S(2)}) collective-permute-start(bf16[768,256]{1,0:T(8,128)(2,1)} %get-tuple-element.33), channel_id=1, source_target_pairs={{0,64},{32,96},{64,0},{96,32},{1,65},{33,97},{65,1},{97,33},{2,66}... | collective-permute-start | bytes 1179656 | tf_op jit(solution)/shard_map/ppermute | solution.py:367
  101.0 0.7 copy-start.4
  101.8 20.5 %copy-start.2 = (bf16[768,256]{1,0:T(8,128)(2,1)S(1)}, bf16[768,256]{1,0:T(8,128)(2,1)}, u32[]{:S(2)}) copy-start(bf16[768,256]{1,0:T(8,128)(2,1)} %get-tuple-element.31.a) | copy-start | bytes 1179652
  101.8 20.5 %collective-permute-start.5 = (bf16[768,256]{1,0:T(8,128)(2,1)}, bf16[768,256]{1,0:T(8,128)(2,1)S(1)}, u32[]{:S(2)}, u32[]{:S(2)}) collective-permute-start(bf16[768,256]{1,0:T(8,128)(2,1)} %get-tuple-element.34), channel_id=1, source_target_pairs={{0,96},{32,64},{64,32},{96,0},{1,97},{33,65},{65,33},{97,1},{2,98}... | collective-permute-start | bytes 1179656 | tf_op jit(solution)/shard_map/ppermute | solution.py:367
  116.2 1.0 copy-start.5

commit v4 on v3

--- a/solution.py
+++ b/solution.py
@@ -30,7 +30,7 @@
 EPS = 1e-06
 VMEM = 56 * 1024 * 1024
 VMEM_LESS = 46 * 1024 * 1024
-VMEM_LEAST = 40 * 1024 * 1024
+VMEM_MID = 50 * 1024 * 1024
 LONG = pl.CostEstimate(flops=40 * 10**9, bytes_accessed=10**8, transcendentals=0)
 
 f32 = jnp.float32
@@ -49,9 +49,15 @@
     place = row // (TM * rows) * BAND + row // rows % TM * (2 * BAND)
     frequency = place + row % rows // (2 * GROUP) * GROUP + row % GROUP
     part = row // GROUP % 2
-    phase = (sample * frequency + part * (WIN // 4)) % WIN
+    phase = jnp.bitwise_and(sample * frequency + part * (WIN // 4), WIN - 1)
+    turn = WIN // 4 - jnp.abs(phase - WIN // 2)
+    angle = turn.astype(f32) * (2.0 * math.pi / WIN)
+    square = angle * angle
+    series = jnp.full_like(square, -1.0 / math.factorial(11))
+    for power in (9, 7, 5, 3, 1):
+        series = series * square + (-1.0) ** (power // 2) / math.factorial(power)
     taper = 0.5 - 0.5 * jnp.cos((sample.astype(f32) + 0.5) * (2.0 * math.pi / WIN))
-    table = taper * jnp.cos(phase.astype(f32) * (2.0 * math.pi / WIN))
+    table = taper * (-angle * series)
     table = lax.optimization_barrier(table).reshape(2, BINS, WIN)
     high = lax.reduce_precision(table, 8, 7)
     return jnp.concatenate([high.astype(bf16), (table - high).astype(bf16)], 1)
@@ -145,6 +151,10 @@
 
 
 def transform_kernel(mine, codes, extra, table, live, *rest):
+    both = len(rest) > TM + 2
+    if both:
+        live_source, rest = rest[0], rest[1:]
+        spectra, (x, bands), rest = rest[TM : 2 * TM], rest[-2:], rest[:TM] + rest[2 * TM : -2]
     outs, (scale, white) = rest[:-2], rest[-2:]
     step = pl.program_id(0)
     rows = 2 * BAND
@@ -152,6 +162,8 @@
 
     @pl.when(step == 0)
     def _():
+        if both:
+            transform_sources(mine, extra, table, live_source, spectra, x, bands)
         scale[...] = scale_of(extra[...].astype(jnp.int32).astype(f32)[:, 8:, :])
 
     for v in range(batch):
@@ -169,35 +181,44 @@
             outs[k][v * rows : (v + 1) * rows, :] = white[jnp.bitwise_xor(mine[0], k)]
 
 
-def transform(mine, received, table, live, band):
+def transform(mine, received, table, live, band, live_source=None):
     rows = 2 * BAND
     batch = 2
-    piece = pl.BlockSpec((batch * rows, WIDTH), lambda w, _: (w, 0))
-    out_specs = [piece] * TM
+    both = live_source is not None
+    in_specs = [
+        pl.BlockSpec((CHAN, batch * SUB, WIDTH), lambda w, _: (0, w, 0)),
+        pl.BlockSpec((CHAN, 16, WIDTH), lambda w, _: (0, DATA // 16, 0)),
+        pl.BlockSpec((2 if both else 1, 2 * BINS, WIN), lambda w, _: (band, 0, 0)),
+        pl.BlockSpec((1, WIDTH), lambda w, _: (0, 0)),
+    ]
+    inputs = [received, received, table, live]
+    out_specs = [pl.BlockSpec((batch * rows, WIDTH), lambda w, _: (w, 0))] * TM
     shapes = [jax.ShapeDtypeStruct((KW * rows, WIDTH), bf16)] * TM
-    return pl.pallas_call(
+    scratch = [pltpu.VMEM((CHAN, 8, WIDTH), f32), pltpu.VMEM((TM, rows, WIDTH), bf16)]
+    if both:
+        in_specs += [pl.BlockSpec((KW * PICK, 1), lambda w, _: (0, 0))]
+        inputs += [live_source]
+        out_specs += [pl.BlockSpec((KW * PICK, 2 * rows), lambda w, _: (0, 0))] * TM
+        shapes += [jax.ShapeDtypeStruct((KW * PICK, 2 * rows), bf16)] * TM
+        scratch += [pltpu.VMEM((KW * PICK, WIN), f32), pltpu.VMEM((2, TM, KW * PICK, rows), f32)]
+    outs = pl.pallas_call(
         transform_kernel,
         grid_spec=pltpu.PrefetchScalarGridSpec(
             num_scalar_prefetch=1,
             grid=(KW // batch,),
-            in_specs=[
-                pl.BlockSpec((CHAN, batch * SUB, WIDTH), lambda w, _: (0, w, 0)),
-                pl.BlockSpec((CHAN, 16, WIDTH), lambda w, _: (0, DATA // 16, 0)),
-                pl.BlockSpec((1, 2 * BINS, WIN), lambda w, _: (band, 0, 0)),
-                pl.BlockSpec((1, WIDTH), lambda w, _: (0, 0)),
-            ],
+            in_specs=in_specs,
             out_specs=out_specs,
-            scratch_shapes=[pltpu.VMEM((CHAN, 8, WIDTH), f32), pltpu.VMEM((TM, rows, WIDTH), bf16)],
+            scratch_shapes=scratch,
         ),
         out_shape=shapes,
-        compiler_params=pltpu.CompilerParams(vmem_limit_bytes=VMEM),
+        compiler_params=pltpu.CompilerParams(vmem_limit_bytes=VMEM_MID if both else VMEM),
         cost_estimate=LONG,
         name="transform",
-    )(mine, received, received, table, live)
-
-
-def sources_kernel(mine, extra, table, live, *rest):
-    outs, (x, bands) = rest[:TM], rest[TM:]
+    )(mine, *inputs)
+    return outs[:TM], outs[TM:]
+
+
+def transform_sources(mine, extra, table, live, outs, x, bands):
     for first in range(0, CHAN, 4):
         values = [extra[d].astype(jnp.int32).astype(f32)[:PICK] for d in range(first, first + 4)]
         scales = [scale_of(value[:, DATA : DATA + KW]) for value in values]
@@ -226,26 +247,6 @@
             outs[k][:, b * rows : (b + 1) * rows] = value.astype(bf16)
 
 
-def sources(mine, received, table, live):
-    rows = 2 * BAND
-    piece = pl.BlockSpec((KW * PICK, WIDTH), lambda i: (0, 0))
-    return pl.pallas_call(
-        sources_kernel,
-        grid=(1,),
-        in_specs=[
-            pl.BlockSpec(memory_space=pltpu.SMEM),
-            pl.BlockSpec((CHAN, 16, WIDTH), lambda i: (0, DATA // 16, 0)),
-            pl.BlockSpec((2, 2 * BINS, WIN), lambda i: (0, 0, 0)),
-            pl.BlockSpec((KW * PICK, 1), lambda i: (0, 0)),
-        ],
-        out_specs=[piece] * TM,
-        out_shape=[jax.ShapeDtypeStruct((KW * PICK, WIDTH), bf16)] * TM,
-        scratch_shapes=[pltpu.VMEM((KW * PICK, WIN), f32), pltpu.VMEM((2, TM, KW * PICK, rows), f32)],
-        compiler_params=pltpu.CompilerParams(vmem_limit_bytes=VMEM_LEAST),
-        name="sources",
-    )(mine, received, table, live)
-
-
 def pack_kernel(a, b, c, d, out):
     parts = [u[...].astype(f32) for u in (a, b, c, d)]
     rows = [part[w * PICK : (w + 1) * PICK] for part in parts for w in range(KW)]
@@ -382,14 +383,13 @@
     table = dft_table()
 
     received = lax.all_to_all(encode(samples, source_index), "chan", 0, 0, tiled=True)
-    spectra = sources(mine, received, table, live_source)
+    pieces, spectra = transform(mine, received, table, live, 0, live_source)
     spectra = [spectra[0]] + [swap(spectra[k], "tm", TM, k) for k in range(1, TM)]
-    pieces = transform(mine, after(received, spectra[0]), table, live, 0)
-    first = [pieces[0]] + [swap(after(pieces[k], *spectra[1:]), "tm", TM, k) for k in range(1, TM)]
-    packed = pack([after(spectra[0], pieces[0])] + spectra[1:])
+    first = [pieces[0]] + [swap(after(pieces[k], spectra[1]), "tm", TM, k) for k in range(1, TM)]
+    packed = pack(spectra)
     groups = [[x * 8 + z * 4 + y for x in range(4) for y in range(4)] for z in range(2)]
     left = lax.all_to_all(packed, "chan", 0, 0, tiled=True, axis_index_groups=groups)
-    pieces = transform(mine, after(received, packed), table, live, 1)
+    pieces, _ = transform(mine, after(received, packed), table, live, 1)
     second = [pieces[0]] + [
         swap(pieces[k], "tm", TM, k) for k in range(1, TM)
     ]

time: 127 us -> 122 us (0.961)
  waiting for transfers between devices: 39.6 us -> 52.9 us
  other arithmetic: 19.3 us -> 7.08 us
  local copies, waits for them, and re-layouts: 6.52 us -> 0.81 us
    all_to_all x1, waiting for transfers between devices: 25.8 us -> 38.6 us  [shards(): lax.all_to_all(encode(samples, source_index), 'chan', 0, 0, tiled=True)]
    mul x1, other arithmetic: 15.8 us -> 3.53 us  [dft_table(): table = taper * (-angle * series)]
    unnamed x16 -> x8, local copies, waits for them, and re-layouts: 5.18 us -> 0.02 us
    pallas_call x2, Pallas kernels: 17.7 us -> 20.7 us  [transform(): pl.pallas_call(transform_kernel, grid_spec=pltpu.PrefetchScalarGridSpec(n...]
    pallas_call x1 -> x0, Pallas kernels: 2.55 us -> none  [sources(): pl.pallas_call(sources_kernel, grid=(1,), in_specs=[pl.BlockSpec(memory_s...]
  transfers between devices with their start and end apart: 11 -> 11, of which waited for: 2 -> 4; matrix products, arithmetic and copies ran while one was open for 16% -> 6% of each run, Pallas kernels for 19% -> 13%
where the time goes in v4:
time: 122 us
  waiting for transfers between devices  52.9 us (43%)
  Pallas kernels  38.4 us (31%)
  starting transfers between devices  22.3 us (18%)
  other arithmetic  7.08 us (6%)
    all_to_all x1, waiting for transfers between devices, shards(): lax.all_to_all(encode(samples, source_index), 'chan', 0, 0, tiled=True)  38.6 us
    pallas_call x2, Pallas kernels, transform(): pl.pallas_call(transform_kernel, grid_spec=pltpu.PrefetchScalarGridSpec(n...  20.7 us
    all_to_all x1, waiting for transfers between devices, shards(): lax.all_to_all(packed, 'chan', 0, 0, tiled=True, axis_index_groups=groups)  13.7 us
    all_to_all x1, starting transfers between devices, shards(): lax.all_to_all(encode(samples, source_index), 'chan', 0, 0, tiled=True)  10.8 us
    pallas_call x2, Pallas kernels, stack(): pl.pallas_call(functools.partial(stack_kernel, band), grid=(1,), in_specs...  8.92 us
    pallas_call x1, Pallas kernels, encode(): pl.pallas_call(encode_kernel, grid=(steps,), in_specs=[pl.BlockSpec((KW,...  7.1 us
    all_to_all x1, starting transfers between devices, shards(): lax.all_to_all(packed, 'chan', 0, 0, tiled=True, axis_index_groups=groups)  5.91 us
    ppermute x9, starting transfers between devices, swap(): return lax.ppermute(value, axis, [(i, i ^ distance) for i in range(size)])  5.6 us
  transfers between devices with their start and end apart: 11, of which 4 were waited for; matrix products, arithmetic and copies ran while one was open for 6% of the time, Pallas kernels for 13%

profile of v4, /device:TPU:0, one launch (start us, length us, event | category | flops | bytes accessed | tf_op | source)
XLA Modules:
  0.0 121.8 jit_solution(989652999182392067)
XLA Ops:
  0.0 7.1 %encode.1 = s16[32,208,256]{2,1,0:T(8,128)(2,1)} custom-call(f32[6,32,8192]{2,1,0:T(8,128)} %samples.1, s32[1,128]{1,0:T(1,128)} %bitcast.7), custom_call_target="tpu_custom_call" | custom-call | tf_op jit(solution)/shard_map/encode/pallas_call | solution.py:133
  7.1 0.0 copy-start.3
  7.1 0.0 copy-start.2
  7.1 10.8 %all-to-all-start = ((s16[32,208,256]{2,1,0:T(8,128)(2,1)}), s16[32,208,256]{2,1,0:T(8,128)(2,1)}, u32[]{:S(2)}, u32[]{:S(2)}) async-start(s16[32,208,256]{2,1,0:T(8,128)(2,1)} %encode.1), calls=%async_computation | async-start | bytes 6815744 | tf_op jit(solution)/shard_map/all_to_all | solution.py:385
  18.0 0.0 copy-done.3
  18.0 0.1 compare_select_fusion
  18.1 0.0 copy-done.2
  18.1 0.6 gather_fusion
  18.8 0.1 dynamic_slice.6
  18.8 0.0 copy-start.1
  18.8 0.1 reshape_tile.4.rest_0_
  19.0 3.5 %multiply_multiply_fusion = f32[1024,1024]{1,0:T(8,128)S(1)} fusion(s32[1024]{0:T(1024)S(1)} %get-tuple-element.40, s32[1024]{0:T(1024)S(1)} %get-tuple-element.39, f32[1024]{0:T(1024)S(1)} %multiply_subtract_fusion), kind=kLoop, calls=%fused_computation.5 | loop fusion | flops 23068672 | bytes 4206592 | tf_op jit(solution)/shard_map/mul | solution.py:60
  22.5 0.9 reduce-precision_convert_fusion
  23.5 2.5 %pad_maximum_fusion.table = bf16[2,1024,1024]{2,1,0:T(8,128)(2,1)} fusion(bf16[2,512,1024]{2,1,0:T(8,128)(2,1)S(1)} %get-tuple-element.38, bf16[2,512,1024]{2,1,0:T(8,128)(2,1)S(1)} %get-tuple-element.37), kind=kLoop, calls=%fused_computation.4 | loop fusion | flops 8388608 | bytes 8388608 | tf_op jit(solution)/shard_map/concatenate | solution.py:63
  25.9 38.6 %all-to-all-done.codes.extra = s16[32,208,256]{2,1,0:T(8,128)(2,1)} async-done(((s16[32,208,256]{2,1,0:T(8,128)(2,1)}), s16[32,208,256]{2,1,0:T(8,128)(2,1)}, u32[]{:S(2)}, u32[]{:S(2)}) %all-to-all-start) | async-done | bytes 3407904 | tf_op jit(solution)/shard_map/all_to_all | solution.py:385
  64.5 0.0 copy-done.1
  64.5 11.8 %transform.2 = (bf16[768,256]{1,0:T(8,128)(2,1)S(1)}, bf16[768,256]{1,0:T(8,128)(2,1)S(1)}, bf16[768,256]{1,0:T(8,128)(2,1)}, bf16[768,256]{1,0:T(8,128)(2,1)}, ...) custom-call(s32[1]{0:T(128)} %bitcast.mine, ...), custom_call_target="tpu_custom_call" | custom-call | flops 40000000000 | bytes 100000000 | tf_op jit(solution)/shard_map/transform/pallas_call | solution.py:204
  76.3 0.0 collective-permute-start
  76.3 1.1 collective-permute-start.1
  77.4 0.8 collective-permute-start.2
  78.2 0.0 collective-permute-done.b
  78.2 0.3 collective-permute-start.6
  78.5 1.0 collective-permute-start.7
  79.6 0.5 collective-permute-start.8
  80.1 0.1 collective-permute-done.1.c
  80.2 0.4 collective-permute-done.2.d
  80.7 1.7 %pack.1 = bf16[16,2,192,128]{3,2,1,0:T(8,128)(2,1)} custom-call(bf16[48,256]{1,0:T(8,128)(2,1)S(1)} %get-tuple-element.21.a, bf16[48,256]{1,0:T(8,128)(2,1)S(1)} %collective-permute-done.b, bf16[48,256]{1,0:T(8,128)(2,1)S(1)} %collective-permute-done.1.c, bf16[48,256]{1,0:T(8,128)(2,1)S(1)} %collective-permute-done.2.d), custom_call_target="tpu_custom_call" | custom-call | tf_op jit(solution)/shard_map/pack/pallas_call | solution.py:275
  82.3 5.9 %all-to-all-start.1 = ((bf16[16,2,192,128]{3,2,1,0:T(8,128)(2,1)}), bf16[16,2,192,128]{3,2,1,0:T(8,128)(2,1)S(1)}, u32[]{:S(2)}, u32[]{:S(2)}) async-start(bf16[16,2,192,128]{3,2,1,0:T(8,128)(2,1)} %pack.1), calls=%async_computation.1 | async-start | bytes 3145728 | tf_op jit(solution)/shard_map/all_to_all | solution.py:391
  88.2 8.9 %transform.3 = (bf16[768,256]{1,0:T(8,128)(2,1)}, bf16[768,256]{1,0:T(8,128)(2,1)}, bf16[768,256]{1,0:T(8,128)(2,1)}, bf16[768,256]{1,0:T(8,128)(2,1)}) custom-call(s32[1]{0:T(128)} %bitcast.mine, s16[32,208,256]{2,1,0:T(8,128)(2,1)} %all-to-all-done.codes.extra, s16[32,208,256]{2,1,0:T(8,128)(2,1)} %all-to-all-done.codes.extra, ...), custom_call_target="tpu_custom_call" | custom-call | flops 40000000000 | bytes 100000000 | tf_op jit(solution)/shard_map/transform/pallas_call | solution.py:204
  97.1 0.0 collective-permute-start.3
  97.1 1.1 collective-permute-start.4
  98.2 0.0 collective-permute-done.6.b
  98.2 0.8 collective-permute-start.5
  99.0 0.0 collective-permute-done.7.c
  99.0 0.0 collective-permute-done.8.d
  99.0 13.7 %all-to-all-done.1.sources = bf16[16,2,192,128]{3,2,1,0:T(8,128)(2,1)S(1)} async-done(((bf16[16,2,192,128]{3,2,1,0:T(8,128)(2,1)}), bf16[16,2,192,128]{3,2,1,0:T(8,128)(2,1)S(1)}, u32[]{:S(2)}, u32[]{:S(2)}) %all-to-all-start.1) | async-done | bytes 1572896 | tf_op jit(solution)/shard_map/all_to_all | solution.py:391
  112.7 0.0 copy-start
  112.7 5.0 %stack.2.rest_0_ = bf16[128,2,128,256]{3,2,1,0:T(8,128)(2,1)} custom-call(bf16[16,2,192,128]{3,2,1,0:T(8,128)(2,1)S(1)} %all-to-all-done.1.sources, bf16[768,256]{1,0:T(8,128)(2,1)S(1)} %get-tuple-element.30.a, bf16[768,256]{1,0:T(8,128)(2,1)S(1)} %collective-permute-done.6.b, bf16[768,256]{1,0:T(8,128)(2,1)} %collective-permute-done.7.c, ...), custom_call_target="tpu_custom_call" | custom-call | tf_op jit(solution)/shard_map/stack/pallas_call | solution.py:348
  117.7 0.0 collective-permute-done.3.b
  117.8 0.0 collective-permute-done.4.c
  117.8 0.0 collective-permute-done.5.d
  117.8 0.0 copy-done
  117.8 3.9 %stack.3 = bf16[128,2,128,256]{3,2,1,0:T(8,128)(2,1)} custom-call(bf16[16,2,192,128]{3,2,1,0:T(8,128)(2,1)S(1)} %all-to-all-done.1.sources, bf16[768,256]{1,0:T(8,128)(2,1)S(1)} %copy-done, bf16[768,256]{1,0:T(8,128)(2,1)S(1)} %collective-permute-done.3.b, bf16[768,256]{1,0:T(8,128)(2,1)S(1)} %collective-permute-done.4.c, ...), custom_call_target="tpu_custom_call", output_to_operand_aliasing={{}: (5, {})} | custom-call | tf_op jit(solution)/shard_map/stack/pallas_call | solution.py:348
  (5 shorter events, 0.1 us)
Async XLA Ops:
  7.1 10.9 %copy-start.3 = (s32[128]{0:T(128)S(1)}, s32[128]{0:T(128)}, u32[]{:S(2)}) copy-start(s32[128]{0:T(128)} %param.4) | copy-start | bytes 1540
  7.1 11.0 %copy-start.2 = (s32[8192]{0:T(1024)S(1)}, s32[8192]{0:T(1024)}, u32[]{:S(2)}) copy-start(s32[8192]{0:T(1024)} %param.5) | copy-start | bytes 98308
  7.1 57.4 %all-to-all-start = ((s16[32,208,256]{2,1,0:T(8,128)(2,1)}), s16[32,208,256]{2,1,0:T(8,128)(2,1)}, u32[]{:S(2)}, u32[]{:S(2)}) async-start(s16[32,208,256]{2,1,0:T(8,128)(2,1)} %encode.1), calls=%async_computation | async-start | bytes 6815744 | tf_op jit(solution)/shard_map/all_to_all | solution.py:385
  18.8 45.7 %copy-start.1 = (f32[256]{0:T(256)}, f32[256]{0:T(256)S(1)}, u32[]{:S(2)}) copy-start(f32[256]{0:T(256)S(1)} %dynamic_slice.6) | copy-start | bytes 3076
  76.3 1.9 %collective-permute-start = (bf16[48,256]{1,0:T(8,128)(2,1)S(1)}, bf16[48,256]{1,0:T(8,128)(2,1)S(1)}, u32[]{:S(2)}, u32[]{:S(2)}) collective-permute-start(bf16[48,256]{1,0:T(8,128)(2,1)S(1)} %get-tuple-element.22), channel_id=1, source_target_pairs={{0,32},{32,0},{64,96},{96,64},{1,33},{33,1},{65,97},{97,65},{2,34}... | collective-permute-start | bytes 73736 | tf_op jit(solution)/shard_map/ppermute | solution.py:368
  76.3 3.9 %collective-permute-start.1 = (bf16[48,256]{1,0:T(8,128)(2,1)S(1)}, bf16[48,256]{1,0:T(8,128)(2,1)S(1)}, u32[]{:S(2)}, u32[]{:S(2)}) collective-permute-start(bf16[48,256]{1,0:T(8,128)(2,1)S(1)} %get-tuple-element.23), channel_id=1, source_target_pairs={{0,64},{32,96},{64,0},{96,32},{1,65},{33,97},{65,1},{97,33},{2,66}... | collective-permute-start | bytes 73736 | tf_op jit(solution)/shard_map/ppermute | solution.py:368
  77.4 3.3 %collective-permute-start.2 = (bf16[48,256]{1,0:T(8,128)(2,1)S(1)}, bf16[48,256]{1,0:T(8,128)(2,1)S(1)}, u32[]{:S(2)}, u32[]{:S(2)}) collective-permute-start(bf16[48,256]{1,0:T(8,128)(2,1)S(1)} %get-tuple-element.24), channel_id=1, source_target_pairs={{0,96},{32,64},{64,32},{96,0},{1,97},{33,65},{65,33},{97,1},{2,98}... | collective-permute-start | bytes 73736 | tf_op jit(solution)/shard_map/ppermute | solution.py:368
  78.2 20.0 %collective-permute-start.6 = (bf16[768,256]{1,0:T(8,128)(2,1)S(1)}, bf16[768,256]{1,0:T(8,128)(2,1)S(1)}, u32[]{:S(2)}, u32[]{:S(2)}) collective-permute-start(bf16[768,256]{1,0:T(8,128)(2,1)S(1)} %get-tuple-element.32), channel_id=1, source_target_pairs={{0,32},{32,0},{64,96},{96,64},{1,33},{33,1},{65,97},{97,65},{2,34}... | collective-permute-start | bytes 1179656 | tf_op jit(solution)/shard_map/ppermute | solution.py:368
  78.5 20.4 %collective-permute-start.7 = (bf16[768,256]{1,0:T(8,128)(2,1)}, bf16[768,256]{1,0:T(8,128)(2,1)}, u32[]{:S(2)}, u32[]{:S(2)}) collective-permute-start(bf16[768,256]{1,0:T(8,128)(2,1)} %get-tuple-element.34), channel_id=1, source_target_pairs={{0,64},{32,96},{64,0},{96,32},{1,65},{33,97},{65,1},{97,33},{2,66}... | collective-permute-start | bytes 1179656 | tf_op jit(solution)/shard_map/ppermute | solution.py:368
  79.6 19.4 %collective-permute-start.8 = (bf16[768,256]{1,0:T(8,128)(2,1)}, bf16[768,256]{1,0:T(8,128)(2,1)}, u32[]{:S(2)}, u32[]{:S(2)}) collective-permute-start(bf16[768,256]{1,0:T(8,128)(2,1)} %get-tuple-element.36), channel_id=1, source_target_pairs={{0,96},{32,64},{64,32},{96,0},{1,97},{33,65},{65,33},{97,1},{2,98}... | collective-permute-start | bytes 1179656 | tf_op jit(solution)/shard_map/ppermute | solution.py:368
  82.3 30.4 %all-to-all-start.1 = ((bf16[16,2,192,128]{3,2,1,0:T(8,128)(2,1)}), bf16[16,2,192,128]{3,2,1,0:T(8,128)(2,1)S(1)}, u32[]{:S(2)}, u32[]{:S(2)}) async-start(bf16[16,2,192,128]{3,2,1,0:T(8,128)(2,1)} %pack.1), calls=%async_computation.1 | async-start | bytes 3145728 | tf_op jit(solution)/shard_map/all_to_all | solution.py:391
  97.1 20.6 %collective-permute-start.3 = (bf16[768,256]{1,0:T(8,128)(2,1)}, bf16[768,256]{1,0:T(8,128)(2,1)S(1)}, u32[]{:S(2)}, u32[]{:S(2)}) collective-permute-start(bf16[768,256]{1,0:T(8,128)(2,1)} %get-tuple-element.27), channel_id=1, source_target_pairs={{0,32},{32,0},{64,96},{96,64},{1,33},{33,1},{65,97},{97,65},{2,34}... | collective-permute-start | bytes 1179656 | tf_op jit(solution)/shard_map/ppermute | solution.py:368
  97.1 20.7 %collective-permute-start.4 = (bf16[768,256]{1,0:T(8,128)(2,1)}, bf16[768,256]{1,0:T(8,128)(2,1)S(1)}, u32[]{:S(2)}, u32[]{:S(2)}) collective-permute-start(bf16[768,256]{1,0:T(8,128)(2,1)} %get-tuple-element.28), channel_id=1, source_target_pairs={{0,64},{32,96},{64,0},{96,32},{1,65},{33,97},{65,1},{97,33},{2,66}... | collective-permute-start | bytes 1179656 | tf_op jit(solution)/shard_map/ppermute | solution.py:368
  98.2 19.6 %collective-permute-start.5 = (bf16[768,256]{1,0:T(8,128)(2,1)}, bf16[768,256]{1,0:T(8,128)(2,1)S(1)}, u32[]{:S(2)}, u32[]{:S(2)}) collective-permute-start(bf16[768,256]{1,0:T(8,128)(2,1)} %get-tuple-element.29), channel_id=1, source_target_pairs={{0,96},{32,64},{64,32},{96,0},{1,97},{33,65},{65,33},{97,1},{2,98}... | collective-permute-start | bytes 1179656 | tf_op jit(solution)/shard_map/ppermute | solution.py:368
  112.7 5.1 %copy-start = (bf16[768,256]{1,0:T(8,128)(2,1)S(1)}, bf16[768,256]{1,0:T(8,128)(2,1)}, u32[]{:S(2)}) copy-start(bf16[768,256]{1,0:T(8,128)(2,1)} %get-tuple-element.26.a) | copy-start | bytes 1179652

commit v5 on v4

--- a/solution.py
+++ b/solution.py
@@ -128,7 +128,7 @@
 
 
 def encode(samples, source_index):
-    wide = 2048
+    wide = 4096
     steps = samples.shape[2] // wide
     return pl.pallas_call(
         encode_kernel,

time: 122 us -> 122 us (level)
  no operation moved by 1% of the time
where the time goes in v5:
time: 122 us
  waiting for transfers between devices  52.9 us (43%)
  Pallas kernels  38.1 us (31%)
  starting transfers between devices  22.4 us (18%)
  other arithmetic  7.08 us (6%)
    all_to_all x1, waiting for transfers between devices, shards(): lax.all_to_all(encode(samples, source_index), 'chan', 0, 0, tiled=True)  38.6 us
    pallas_call x2, Pallas kernels, transform(): pl.pallas_call(transform_kernel, grid_spec=pltpu.PrefetchScalarGridSpec(n...  20.7 us
    all_to_all x1, waiting for transfers between devices, shards(): lax.all_to_all(packed, 'chan', 0, 0, tiled=True, axis_index_groups=groups)  13.7 us
    all_to_all x1, starting transfers between devices, shards(): lax.all_to_all(encode(samples, source_index), 'chan', 0, 0, tiled=True)  10.8 us
    pallas_call x2, Pallas kernels, stack(): pl.pallas_call(functools.partial(stack_kernel, band), grid=(1,), in_specs...  8.92 us
    pallas_call x1, Pallas kernels, encode(): pl.pallas_call(encode_kernel, grid=(steps,), in_specs=[pl.BlockSpec((KW,...  6.87 us
    all_to_all x1, starting transfers between devices, shards(): lax.all_to_all(packed, 'chan', 0, 0, tiled=True, axis_index_groups=groups)  5.92 us
    ppermute x9, starting transfers between devices, swap(): return lax.ppermute(value, axis, [(i, i ^ distance) for i in range(size)])  5.6 us
  transfers between devices with their start and end apart: 11, of which 4 were waited for; matrix products, arithmetic and copies ran while one was open for 6% of the time, Pallas kernels for 13%

profile of v5, /device:TPU:0, one launch (start us, length us, event | category | flops | bytes accessed | tf_op | source)
XLA Modules:
  0.0 121.6 jit_solution(4114608575103061318)
XLA Ops:
  0.0 6.9 %encode.1 = s16[32,208,256]{2,1,0:T(8,128)(2,1)} custom-call(f32[6,32,8192]{2,1,0:T(8,128)} %samples.1, s32[1,128]{1,0:T(1,128)} %bitcast.7), custom_call_target="tpu_custom_call" | custom-call | tf_op jit(solution)/shard_map/encode/pallas_call | solution.py:133
  6.9 0.0 copy-start.3
  6.9 0.0 copy-start.2
  6.9 10.8 %all-to-all-start = ((s16[32,208,256]{2,1,0:T(8,128)(2,1)}), s16[32,208,256]{2,1,0:T(8,128)(2,1)}, u32[]{:S(2)}, u32[]{:S(2)}) async-start(s16[32,208,256]{2,1,0:T(8,128)(2,1)} %encode.1), calls=%async_computation | async-start | bytes 6815744 | tf_op jit(solution)/shard_map/all_to_all | solution.py:385
  17.8 0.0 copy-done.3
  17.8 0.1 compare_select_fusion
  17.9 0.0 copy-done.2
  17.9 0.6 gather_fusion
  18.5 0.1 dynamic_slice.6
  18.6 0.0 copy-start.1
  18.6 0.1 reshape_tile.4.rest_0_
  18.8 3.5 %multiply_multiply_fusion = f32[1024,1024]{1,0:T(8,128)S(1)} fusion(s32[1024]{0:T(1024)S(1)} %get-tuple-element.40, s32[1024]{0:T(1024)S(1)} %get-tuple-element.39, f32[1024]{0:T(1024)S(1)} %multiply_subtract_fusion), kind=kLoop, calls=%fused_computation.5 | loop fusion | flops 23068672 | bytes 4206592 | tf_op jit(solution)/shard_map/mul | solution.py:60
  22.3 0.9 reduce-precision_convert_fusion
  23.2 2.5 %pad_maximum_fusion.table = bf16[2,1024,1024]{2,1,0:T(8,128)(2,1)} fusion(bf16[2,512,1024]{2,1,0:T(8,128)(2,1)S(1)} %get-tuple-element.38, bf16[2,512,1024]{2,1,0:T(8,128)(2,1)S(1)} %get-tuple-element.37), kind=kLoop, calls=%fused_computation.4 | loop fusion | flops 8388608 | bytes 8388608 | tf_op jit(solution)/shard_map/concatenate | solution.py:63
  25.7 38.6 %all-to-all-done.codes.extra = s16[32,208,256]{2,1,0:T(8,128)(2,1)} async-done(((s16[32,208,256]{2,1,0:T(8,128)(2,1)}), s16[32,208,256]{2,1,0:T(8,128)(2,1)}, u32[]{:S(2)}, u32[]{:S(2)}) %all-to-all-start) | async-done | bytes 3407904 | tf_op jit(solution)/shard_map/all_to_all | solution.py:385
  64.3 0.0 copy-done.1
  64.3 11.8 %transform.2 = (bf16[768,256]{1,0:T(8,128)(2,1)S(1)}, bf16[768,256]{1,0:T(8,128)(2,1)S(1)}, bf16[768,256]{1,0:T(8,128)(2,1)}, bf16[768,256]{1,0:T(8,128)(2,1)}, ...) custom-call(s32[1]{0:T(128)} %bitcast.mine, ...), custom_call_target="tpu_custom_call" | custom-call | flops 40000000000 | bytes 100000000 | tf_op jit(solution)/shard_map/transform/pallas_call | solution.py:204
  76.1 0.0 collective-permute-start
  76.1 1.1 collective-permute-start.1
  77.2 0.8 collective-permute-start.2
  78.0 0.0 collective-permute-done.b
  78.0 0.3 collective-permute-start.6
  78.3 1.0 collective-permute-start.7
  79.3 0.5 collective-permute-start.8
  79.9 0.1 collective-permute-done.1.c
  80.0 0.4 collective-permute-done.2.d
  80.4 1.7 %pack.1 = bf16[16,2,192,128]{3,2,1,0:T(8,128)(2,1)} custom-call(bf16[48,256]{1,0:T(8,128)(2,1)S(1)} %get-tuple-element.21.a, bf16[48,256]{1,0:T(8,128)(2,1)S(1)} %collective-permute-done.b, bf16[48,256]{1,0:T(8,128)(2,1)S(1)} %collective-permute-done.1.c, bf16[48,256]{1,0:T(8,128)(2,1)S(1)} %collective-permute-done.2.d), custom_call_target="tpu_custom_call" | custom-call | tf_op jit(solution)/shard_map/pack/pallas_call | solution.py:275
  82.1 5.9 %all-to-all-start.1 = ((bf16[16,2,192,128]{3,2,1,0:T(8,128)(2,1)}), bf16[16,2,192,128]{3,2,1,0:T(8,128)(2,1)S(1)}, u32[]{:S(2)}, u32[]{:S(2)}) async-start(bf16[16,2,192,128]{3,2,1,0:T(8,128)(2,1)} %pack.1), calls=%async_computation.1 | async-start | bytes 3145728 | tf_op jit(solution)/shard_map/all_to_all | solution.py:391
  88.0 8.9 %transform.3 = (bf16[768,256]{1,0:T(8,128)(2,1)}, bf16[768,256]{1,0:T(8,128)(2,1)}, bf16[768,256]{1,0:T(8,128)(2,1)}, bf16[768,256]{1,0:T(8,128)(2,1)}) custom-call(s32[1]{0:T(128)} %bitcast.mine, s16[32,208,256]{2,1,0:T(8,128)(2,1)} %all-to-all-done.codes.extra, s16[32,208,256]{2,1,0:T(8,128)(2,1)} %all-to-all-done.codes.extra, ...), custom_call_target="tpu_custom_call" | custom-call | flops 40000000000 | bytes 100000000 | tf_op jit(solution)/shard_map/transform/pallas_call | solution.py:204
  96.9 0.0 collective-permute-start.3
  96.9 1.1 collective-permute-start.4
  98.0 0.0 collective-permute-done.6.b
  98.0 0.8 collective-permute-start.5
  98.8 0.0 collective-permute-done.7.c
  98.8 0.0 collective-permute-done.8.d
  98.8 13.7 %all-to-all-done.1.sources = bf16[16,2,192,128]{3,2,1,0:T(8,128)(2,1)S(1)} async-done(((bf16[16,2,192,128]{3,2,1,0:T(8,128)(2,1)}), bf16[16,2,192,128]{3,2,1,0:T(8,128)(2,1)S(1)}, u32[]{:S(2)}, u32[]{:S(2)}) %all-to-all-start.1) | async-done | bytes 1572896 | tf_op jit(solution)/shard_map/all_to_all | solution.py:391
  112.5 0.0 copy-start
  112.5 5.0 %stack.2.rest_0_ = bf16[128,2,128,256]{3,2,1,0:T(8,128)(2,1)} custom-call(bf16[16,2,192,128]{3,2,1,0:T(8,128)(2,1)S(1)} %all-to-all-done.1.sources, bf16[768,256]{1,0:T(8,128)(2,1)S(1)} %get-tuple-element.30.a, bf16[768,256]{1,0:T(8,128)(2,1)S(1)} %collective-permute-done.6.b, bf16[768,256]{1,0:T(8,128)(2,1)} %collective-permute-done.7.c, ...), custom_call_target="tpu_custom_call" | custom-call | tf_op jit(solution)/shard_map/stack/pallas_call | solution.py:348
  117.5 0.0 collective-permute-done.3.b
  117.5 0.0 collective-permute-done.4.c
  117.6 0.0 collective-permute-done.5.d
  117.6 0.0 copy-done
  117.6 3.9 %stack.3 = bf16[128,2,128,256]{3,2,1,0:T(8,128)(2,1)} custom-call(bf16[16,2,192,128]{3,2,1,0:T(8,128)(2,1)S(1)} %all-to-all-done.1.sources, bf16[768,256]{1,0:T(8,128)(2,1)S(1)} %copy-done, bf16[768,256]{1,0:T(8,128)(2,1)S(1)} %collective-permute-done.3.b, bf16[768,256]{1,0:T(8,128)(2,1)S(1)} %collective-permute-done.4.c, ...), custom_call_target="tpu_custom_call", output_to_operand_aliasing={{}: (5, {})} | custom-call | tf_op jit(solution)/shard_map/stack/pallas_call | solution.py:348
  (5 shorter events, 0.1 us)
Async XLA Ops:
  6.9 10.9 %copy-start.3 = (s32[128]{0:T(128)S(1)}, s32[128]{0:T(128)}, u32[]{:S(2)}) copy-start(s32[128]{0:T(128)} %param.4) | copy-start | bytes 1540
  6.9 11.0 %copy-start.2 = (s32[8192]{0:T(1024)S(1)}, s32[8192]{0:T(1024)}, u32[]{:S(2)}) copy-start(s32[8192]{0:T(1024)} %param.5) | copy-start | bytes 98308
  6.9 57.4 %all-to-all-start = ((s16[32,208,256]{2,1,0:T(8,128)(2,1)}), s16[32,208,256]{2,1,0:T(8,128)(2,1)}, u32[]{:S(2)}, u32[]{:S(2)}) async-start(s16[32,208,256]{2,1,0:T(8,128)(2,1)} %encode.1), calls=%async_computation | async-start | bytes 6815744 | tf_op jit(solution)/shard_map/all_to_all | solution.py:385
  18.6 45.7 %copy-start.1 = (f32[256]{0:T(256)}, f32[256]{0:T(256)S(1)}, u32[]{:S(2)}) copy-start(f32[256]{0:T(256)S(1)} %dynamic_slice.6) | copy-start | bytes 3076
  76.1 1.9 %collective-permute-start = (bf16[48,256]{1,0:T(8,128)(2,1)S(1)}, bf16[48,256]{1,0:T(8,128)(2,1)S(1)}, u32[]{:S(2)}, u32[]{:S(2)}) collective-permute-start(bf16[48,256]{1,0:T(8,128)(2,1)S(1)} %get-tuple-element.22), channel_id=1, source_target_pairs={{0,32},{32,0},{64,96},{96,64},{1,33},{33,1},{65,97},{97,65},{2,34}... | collective-permute-start | bytes 73736 | tf_op jit(solution)/shard_map/ppermute | solution.py:368
  76.1 3.9 %collective-permute-start.1 = (bf16[48,256]{1,0:T(8,128)(2,1)S(1)}, bf16[48,256]{1,0:T(8,128)(2,1)S(1)}, u32[]{:S(2)}, u32[]{:S(2)}) collective-permute-start(bf16[48,256]{1,0:T(8,128)(2,1)S(1)} %get-tuple-element.23), channel_id=1, source_target_pairs={{0,64},{32,96},{64,0},{96,32},{1,65},{33,97},{65,1},{97,33},{2,66}... | collective-permute-start | bytes 73736 | tf_op jit(solution)/shard_map/ppermute | solution.py:368
  77.2 3.3 %collective-permute-start.2 = (bf16[48,256]{1,0:T(8,128)(2,1)S(1)}, bf16[48,256]{1,0:T(8,128)(2,1)S(1)}, u32[]{:S(2)}, u32[]{:S(2)}) collective-permute-start(bf16[48,256]{1,0:T(8,128)(2,1)S(1)} %get-tuple-element.24), channel_id=1, source_target_pairs={{0,96},{32,64},{64,32},{96,0},{1,97},{33,65},{65,33},{97,1},{2,98}... | collective-permute-start | bytes 73736 | tf_op jit(solution)/shard_map/ppermute | solution.py:368
  78.0 20.0 %collective-permute-start.6 = (bf16[768,256]{1,0:T(8,128)(2,1)S(1)}, bf16[768,256]{1,0:T(8,128)(2,1)S(1)}, u32[]{:S(2)}, u32[]{:S(2)}) collective-permute-start(bf16[768,256]{1,0:T(8,128)(2,1)S(1)} %get-tuple-element.32), channel_id=1, source_target_pairs={{0,32},{32,0},{64,96},{96,64},{1,33},{33,1},{65,97},{97,65},{2,34}... | collective-permute-start | bytes 1179656 | tf_op jit(solution)/shard_map/ppermute | solution.py:368
  78.3 20.4 %collective-permute-start.7 = (bf16[768,256]{1,0:T(8,128)(2,1)}, bf16[768,256]{1,0:T(8,128)(2,1)}, u32[]{:S(2)}, u32[]{:S(2)}) collective-permute-start(bf16[768,256]{1,0:T(8,128)(2,1)} %get-tuple-element.34), channel_id=1, source_target_pairs={{0,64},{32,96},{64,0},{96,32},{1,65},{33,97},{65,1},{97,33},{2,66}... | collective-permute-start | bytes 1179656 | tf_op jit(solution)/shard_map/ppermute | solution.py:368
  79.3 19.4 %collective-permute-start.8 = (bf16[768,256]{1,0:T(8,128)(2,1)}, bf16[768,256]{1,0:T(8,128)(2,1)}, u32[]{:S(2)}, u32[]{:S(2)}) collective-permute-start(bf16[768,256]{1,0:T(8,128)(2,1)} %get-tuple-element.36), channel_id=1, source_target_pairs={{0,96},{32,64},{64,32},{96,0},{1,97},{33,65},{65,33},{97,1},{2,98}... | collective-permute-start | bytes 1179656 | tf_op jit(solution)/shard_map/ppermute | solution.py:368
  82.1 30.4 %all-to-all-start.1 = ((bf16[16,2,192,128]{3,2,1,0:T(8,128)(2,1)}), bf16[16,2,192,128]{3,2,1,0:T(8,128)(2,1)S(1)}, u32[]{:S(2)}, u32[]{:S(2)}) async-start(bf16[16,2,192,128]{3,2,1,0:T(8,128)(2,1)} %pack.1), calls=%async_computation.1 | async-start | bytes 3145728 | tf_op jit(solution)/shard_map/all_to_all | solution.py:391
  96.9 20.6 %collective-permute-start.3 = (bf16[768,256]{1,0:T(8,128)(2,1)}, bf16[768,256]{1,0:T(8,128)(2,1)S(1)}, u32[]{:S(2)}, u32[]{:S(2)}) collective-permute-start(bf16[768,256]{1,0:T(8,128)(2,1)} %get-tuple-element.27), channel_id=1, source_target_pairs={{0,32},{32,0},{64,96},{96,64},{1,33},{33,1},{65,97},{97,65},{2,34}... | collective-permute-start | bytes 1179656 | tf_op jit(solution)/shard_map/ppermute | solution.py:368
  96.9 20.7 %collective-permute-start.4 = (bf16[768,256]{1,0:T(8,128)(2,1)}, bf16[768,256]{1,0:T(8,128)(2,1)S(1)}, u32[]{:S(2)}, u32[]{:S(2)}) collective-permute-start(bf16[768,256]{1,0:T(8,128)(2,1)} %get-tuple-element.28), channel_id=1, source_target_pairs={{0,64},{32,96},{64,0},{96,32},{1,65},{33,97},{65,1},{97,33},{2,66}... | collective-permute-start | bytes 1179656 | tf_op jit(solution)/shard_map/ppermute | solution.py:368
  98.0 19.6 %collective-permute-start.5 = (bf16[768,256]{1,0:T(8,128)(2,1)}, bf16[768,256]{1,0:T(8,128)(2,1)S(1)}, u32[]{:S(2)}, u32[]{:S(2)}) collective-permute-start(bf16[768,256]{1,0:T(8,128)(2,1)} %get-tuple-element.29), channel_id=1, source_target_pairs={{0,96},{32,64},{64,32},{96,0},{1,97},{33,65},{65,33},{97,1},{2,98}... | collective-permute-start | bytes 1179656 | tf_op jit(solution)/shard_map/ppermute | solution.py:368
  112.5 5.1 %copy-start = (bf16[768,256]{1,0:T(8,128)(2,1)S(1)}, bf16[768,256]{1,0:T(8,128)(2,1)}, u32[]{:S(2)}) copy-start(bf16[768,256]{1,0:T(8,128)(2,1)} %get-tuple-element.26.a) | copy-start | bytes 1179652
